TPU v7x, 128 devices: a whole 4x4x4 slice. The times are simulated.
128 devices in a mesh: pts: 16 (over z_lo, y, core), tau: 8 (over z_hi, x).
Axes of the slice: x: 4, y: 4, z: 4 (z_hi: 2, z_lo: 2; z = z_hi * 2 + z_lo), core: 2. Of those that a mesh axis runs over, the one named last changes fastest.
Arguments:
- occ_orbitals: bfloat16 [6144, 2048], P('pts'), may hold values from -1 to 1
- virt_orbitals: bfloat16 [6144, 4096], P('pts'), may hold values from -1 to 1
- potentials: bfloat16 [6144, 256], P('pts'), may hold values from -1 to 1
- occ_energy: float32 [2048], replicated, may hold values from -1 to -0.1
- virt_energy: float32 [4096], replicated, may hold values from 0.1 to 1
- times: float32 [8], P('tau'), may hold values from 0.25 to 4
- weights: float32 [8, 8], P(None, 'tau'), may hold values from -2 to 2
Outputs:
- screened: float32 [8, 256, 256], P('tau')
All inputs are finite; a program needn't handle non-finite values.
Results may differ from a plain program's by a relative error of at most 0.0003.
Values may be sent and summed in bfloat16 or wider, within the bound.
A program may use at most 128 MiB of HBM per device.

v0:
```python
import jax
import jax.numpy as jnp
from jax import lax
from jax.sharding import PartitionSpec as P


def from_behind(value, axis, steps):
    count = lax.axis_size(axis)
    pairs = [(source, (source + steps) % count) for source in range(count)]
    return lax.ppermute(value, axis, pairs)


def copy_for_each(shard, axis):
    peers = lax.axis_size(axis)
    return lax.all_to_all(
        jnp.broadcast_to(shard[None], (peers, *shard.shape)), axis, 0, 0, tiled=True
    )


def over_copies(shard, axis):
    everything = copy_for_each(shard, axis)
    return jnp.sum(everything, axis=0)


def cut_along(shard, dim, peers):
    dims = shard.shape
    parts = shard.reshape(*dims[:dim], peers, dims[dim] // peers, *dims[dim + 1 :])
    return jnp.moveaxis(parts, dim, 0)


def summed_on_arrival(shard, axis, dim):
    parts = cut_along(shard, dim, lax.axis_size(axis))
    arrived = lax.all_to_all(parts, axis, split_axis=0, concat_axis=0, tiled=True)
    return arrived.sum(axis=0)


def body(occ_orbitals, virt_orbitals, potentials, occ_energy, virt_energy, times, weights):
    cycle_size = lax.axis_size("pts")
    half_cycle = cycle_size // 2
    n_occ = occ_orbitals.shape[1]
    n_virt = virt_orbitals.shape[1]
    moment = times[0]
    occ_factor = jnp.exp(0.5 * moment * occ_energy)
    virt_factor = jnp.exp(-0.5 * moment * virt_energy)
    contract = (((1,), (1,)), ((), ()))
    occ_scaled = (occ_orbitals.astype(jnp.float32) * occ_factor).astype(jnp.bfloat16)
    virt_scaled = (virt_orbitals.astype(jnp.float32) * virt_factor).astype(jnp.bfloat16)
    pot_wide = potentials.astype(jnp.float32)

    def pair_block(far_occ, far_virt, far_pot):
        green_occ = lax.dot_general(
            occ_scaled, far_occ, contract, preferred_element_type=jnp.float32
        )
        green_virt = lax.dot_general(
            virt_scaled, far_virt, contract, preferred_element_type=jnp.float32
        )
        response = (-(green_occ * green_virt)).astype(jnp.bfloat16)
        applied = jnp.dot(response, far_pot, preferred_element_type=jnp.float32)
        return lax.dot_general(
            pot_wide, applied, (((0,), (0,)), ((), ())), precision=lax.Precision.HIGHEST
        )

    parcel = jnp.concatenate([occ_scaled, virt_scaled, potentials], axis=1)
    summed_pairs = pair_block(occ_scaled, virt_scaled, potentials)
    arrived = parcel
    for offset in range(1, half_cycle + 1):
        arrived = from_behind(arrived, "pts", -1)
        far_occ = arrived[:, :n_occ]
        far_virt = arrived[:, n_occ : n_occ + n_virt]
        far_pot = arrived[:, n_occ + n_virt :]
        pair_sum = pair_block(far_occ, far_virt, far_pot)
        if offset < half_cycle:
            summed_pairs = summed_pairs + pair_sum + pair_sum.T
        else:
            summed_pairs = summed_pairs + pair_sum
    all_pairs = over_copies(summed_pairs, "pts")
    weighted = weights[:, 0][:, None, None] * all_pairs[None]
    screened = summed_on_arrival(weighted, "tau", 0)
    return screened


def solution(mesh):
    return jax.shard_map(
        body,
        mesh=mesh,
        in_specs=(
            P("pts", None),
            P("pts", None),
            P("pts", None),
            P(),
            P(),
            P("tau"),
            P(None, "tau"),
        ),
        out_specs=P("tau", None, None),
        check_vma=False,
    )
```

profile of v0, /device:TPU:1, one launch (start us, length us, event | category | flops | bytes accessed | tf_op | source)
XLA Modules:
  0.0 577.1 jit_solution(1537831819614454999)
XLA Ops:
  0.8 0.9 multiply_exponential_fusion.1
  1.7 0.7 multiply_exponential_fusion
  2.4 1.8 multiply_convert_fusion.1
  4.2 0.8 multiply_convert_fusion
  5.0 0.4 copy-done.1
  5.4 0.4 pad_maximum_fusion
  5.7 1.5 collective-permute-start
  7.2 55.2 %collective-permute-done = bf16[384,6400]{1,0:T(8,128)(2,1)S(1)} collective-permute-done((bf16[384,6400]{1,0:T(8,128)(2,1)S(1)}, bf16[384,6400]{1,0:T(8,128)(2,1)S(1)}, u32[]{:S(2)}, u32[]{:S(2)}) %collective-permute-start) | collective-permute-done | bytes 4915232 | tf_op jit(solution)/shard_map/ppermute | solution.py:10
  62.4 2.5 collective-permute-start.1
  64.9 53.2 %collective-permute-done.1 = bf16[384,6400]{1,0:T(8,128)(2,1)S(1)} collective-permute-done((bf16[384,6400]{1,0:T(8,128)(2,1)S(1)}, bf16[384,6400]{1,0:T(8,128)(2,1)S(1)}, u32[]{:S(2)}, u32[]{:S(2)}) %collective-permute-start.1) | collective-permute-done | bytes 4915232 | tf_op jit(solution)/shard_map/ppermute | solution.py:10
  118.1 4.6 collective-permute-start.2
  122.6 51.1 %collective-permute-done.2 = bf16[384,6400]{1,0:T(8,128)(2,1)S(1)} collective-permute-done((bf16[384,6400]{1,0:T(8,128)(2,1)S(1)}, bf16[384,6400]{1,0:T(8,128)(2,1)S(1)}, u32[]{:S(2)}, u32[]{:S(2)}) %collective-permute-start.2) | collective-permute-done | bytes 4915232 | tf_op jit(solution)/shard_map/ppermute | solution.py:10
  173.7 6.7 %collective-permute-start.3 = (bf16[384,6400]{1,0:T(8,128)(2,1)S(1)}, bf16[384,6400]{1,0:T(8,128)(2,1)S(1)}, u32[]{:S(2)}, u32[]{:S(2)}) collective-permute-start(bf16[384,6400]{1,0:T(8,128)(2,1)S(1)} %collective-permute-done.2), channel_id=1, source_target_pairs={{0,120},{8,0},{16,8},{24,16},{32,24},{40,32},{48,40},{56,48},{64,5... | collective-permute-start | bytes 14745608 | tf_op jit(solution)/shard_map/ppermute | solution.py:10
  180.4 49.0 %collective-permute-done.3 = bf16[384,6400]{1,0:T(8,128)(2,1)S(1)} collective-permute-done((bf16[384,6400]{1,0:T(8,128)(2,1)S(1)}, bf16[384,6400]{1,0:T(8,128)(2,1)S(1)}, u32[]{:S(2)}, u32[]{:S(2)}) %collective-permute-start.3) | collective-permute-done | bytes 4915232 | tf_op jit(solution)/shard_map/ppermute | solution.py:10
  229.4 2.2 copy-done.5
  231.5 8.8 %collective-permute-start.4 = (bf16[384,6400]{1,0:T(8,128)(2,1)S(1)}, bf16[384,6400]{1,0:T(8,128)(2,1)S(1)}, u32[]{:S(2)}, u32[]{:S(2)}) collective-permute-start(bf16[384,6400]{1,0:T(8,128)(2,1)S(1)} %collective-permute-done.3), channel_id=1, source_target_pairs={{0,120},{8,0},{16,8},{24,16},{32,24},{40,32},{48,40},{56,48},{64,5... | collective-permute-start | bytes 14745608 | tf_op jit(solution)/shard_map/ppermute | solution.py:10
  240.3 46.9 %collective-permute-done.4 = bf16[384,6400]{1,0:T(8,128)(2,1)S(1)} collective-permute-done((bf16[384,6400]{1,0:T(8,128)(2,1)S(1)}, bf16[384,6400]{1,0:T(8,128)(2,1)S(1)}, u32[]{:S(2)}, u32[]{:S(2)}) %collective-permute-start.4) | collective-permute-done | bytes 4915232 | tf_op jit(solution)/shard_map/ppermute | solution.py:10
  287.2 2.2 copy-done.6
  289.4 10.9 %collective-permute-start.5 = (bf16[384,6400]{1,0:T(8,128)(2,1)S(1)}, bf16[384,6400]{1,0:T(8,128)(2,1)}, u32[]{:S(2)}, u32[]{:S(2)}) collective-permute-start(bf16[384,6400]{1,0:T(8,128)(2,1)S(1)} %collective-permute-done.4), channel_id=1, source_target_pairs={{0,120},{8,0},{16,8},{24,16},{32,24},{40,32},{48,40},{56,48},{64,5... | collective-permute-start | bytes 14745608 | tf_op jit(solution)/shard_map/ppermute | solution.py:10
  300.3 44.9 %collective-permute-done.5 = bf16[384,6400]{1,0:T(8,128)(2,1)} collective-permute-done((bf16[384,6400]{1,0:T(8,128)(2,1)S(1)}, bf16[384,6400]{1,0:T(8,128)(2,1)}, u32[]{:S(2)}, u32[]{:S(2)}) %collective-permute-start.5) | collective-permute-done | bytes 4915232 | tf_op jit(solution)/shard_map/ppermute | solution.py:10
  345.2 12.9 %collective-permute-start.6 = (bf16[384,6400]{1,0:T(8,128)(2,1)}, bf16[384,6400]{1,0:T(8,128)(2,1)}, u32[]{:S(2)}, u32[]{:S(2)}) collective-permute-start(bf16[384,6400]{1,0:T(8,128)(2,1)} %collective-permute-done.5), channel_id=1, source_target_pairs={{0,120},{8,0},{16,8},{24,16},{32,24},{40,32},{48,40},{56,48},{64,5... | collective-permute-start | bytes 14745608 | tf_op jit(solution)/shard_map/ppermute | solution.py:10
  358.1 2.6 fusion.154
  360.7 4.0 fusion.130
  364.7 4.5 fusion.14
  369.2 4.0 fusion.107
  373.3 2.2 fusion.155
  375.5 1.8 copy.16
  377.3 4.6 fusion.12
  381.8 4.0 fusion.110
  385.9 2.2 fusion.156
  388.1 1.8 copy.17
  389.9 4.6 fusion.10
  394.4 4.0 fusion.113
  398.5 2.7 collective-permute-done.6
  401.1 15.1 %collective-permute-start.7 = (bf16[384,6400]{1,0:T(8,128)(2,1)}, bf16[384,6400]{1,0:T(8,128)(2,1)}, u32[]{:S(2)}, u32[]{:S(2)}) collective-permute-start(bf16[384,6400]{1,0:T(8,128)(2,1)} %collective-permute-done.6), channel_id=1, source_target_pairs={{0,120},{8,0},{16,8},{24,16},{32,24},{40,32},{48,40},{56,48},{64,5... | collective-permute-start | bytes 14745608 | tf_op jit(solution)/shard_map/ppermute | solution.py:10
  416.2 2.2 fusion.157
  418.4 1.8 copy.18
  420.2 4.6 fusion.8
  424.8 4.0 fusion.116
  428.8 2.2 fusion.158
  431.0 1.8 copy.19
  432.8 4.5 fusion.6
  437.4 4.0 fusion.119
  441.4 2.2 fusion.159
  443.6 1.8 copy.20
  445.4 4.5 fusion.4
  449.9 4.0 fusion.122
  453.9 2.2 fusion.160
  456.1 1.8 copy.21
  457.9 4.5 fusion.2
  462.4 4.0 fusion.125
  466.5 2.2 fusion.161
  468.7 1.8 copy.22
  470.5 3.4 fusion.145
  473.9 4.8 fusion
  478.7 3.3 fusion.128
  482.0 0.5 fusion.131
  482.5 0.1 copy.23
  482.6 0.4 broadcast_in_dim.2
  483.1 56.5 %all_to_all.10 = f32[16,256,256]{2,1,0:T(8,128)} all-to-all(f32[16,256,256]{2,1,0:T(8,128)S(1)} %broadcast_in_dim.2), channel_id=1, replica_groups=mesh['pts'=16,'tau'=8] {'pts'}, dimensions={0} | all-to-all | bytes 8388608 | tf_op jit(solution)/shard_map/all_to_all | solution.py:15
  539.6 2.5 reduce_sum.20
  542.1 0.2 broadcast_multiply_fusion
  542.3 33.9 %all_to_all.11 = f32[8,1,256,256]{3,2,1,0:T(8,128)S(1)} all-to-all(f32[8,1,256,256]{3,2,1,0:T(8,128)S(1)} %broadcast_multiply_fusion), channel_id=1, replica_groups=mesh['pts'=16,'tau'=8] {'tau'}, dimensions={0} | all-to-all | bytes 4194304 | tf_op jit(solution)/shard_map/all_to_all | solution.py:33
  576.2 0.8 reduce_sum.21
  (18 shorter events, 0.0 us)
Async XLA Ops:
  0.0 4.2 copy-start.2
  4.2 1.1 copy-start.1
  4.2 1.1 copy-start
  5.7 56.7 %collective-permute-start = (bf16[384,6400]{1,0:T(8,128)(2,1)S(1)}, bf16[384,6400]{1,0:T(8,128)(2,1)S(1)}, u32[]{:S(2)}, u32[]{:S(2)}) collective-permute-start(bf16[384,6400]{1,0:T(8,128)(2,1)S(1)} %pad_maximum_fusion), channel_id=1, source_target_pairs={{0,120},{8,0},{16,8},{24,16},{32,24},{40,32},{48,40},{56,48},{64,5... | collective-permute-start | bytes 14745608 | tf_op jit(solution)/shard_map/ppermute | solution.py:10
  62.4 60.2 %copy-start.7 = (bf16[384,6400]{1,0:T(8,128)(2,1)}, bf16[384,6400]{1,0:T(8,128)(2,1)S(1)}, u32[]{:S(2)}) copy-start(bf16[384,6400]{1,0:T(8,128)(2,1)S(1)} %collective-permute-done) | copy-start | bytes 14745604
  62.4 55.7 %collective-permute-start.1 = (bf16[384,6400]{1,0:T(8,128)(2,1)S(1)}, bf16[384,6400]{1,0:T(8,128)(2,1)S(1)}, u32[]{:S(2)}, u32[]{:S(2)}) collective-permute-start(bf16[384,6400]{1,0:T(8,128)(2,1)S(1)} %collective-permute-done), channel_id=1, source_target_pairs={{0,120},{8,0},{16,8},{24,16},{32,24},{40,32},{48,40},{56,48},{64,5... | collective-permute-start | bytes 14745608 | tf_op jit(solution)/shard_map/ppermute | solution.py:10
  118.1 62.3 %copy-start.8 = (bf16[384,6400]{1,0:T(8,128)(2,1)}, bf16[384,6400]{1,0:T(8,128)(2,1)S(1)}, u32[]{:S(2)}) copy-start(bf16[384,6400]{1,0:T(8,128)(2,1)S(1)} %collective-permute-done.1) | copy-start | bytes 14745604
  118.1 55.7 %collective-permute-start.2 = (bf16[384,6400]{1,0:T(8,128)(2,1)S(1)}, bf16[384,6400]{1,0:T(8,128)(2,1)S(1)}, u32[]{:S(2)}, u32[]{:S(2)}) collective-permute-start(bf16[384,6400]{1,0:T(8,128)(2,1)S(1)} %collective-permute-done.1), channel_id=1, source_target_pairs={{0,120},{8,0},{16,8},{24,16},{32,24},{40,32},{48,40},{56,48},{64,5... | collective-permute-start | bytes 14745608 | tf_op jit(solution)/shard_map/ppermute | solution.py:10
  173.7 171.4 %copy-start.9 = (bf16[384,6400]{1,0:T(8,128)(2,1)}, bf16[384,6400]{1,0:T(8,128)(2,1)S(1)}, u32[]{:S(2)}) copy-start(bf16[384,6400]{1,0:T(8,128)(2,1)S(1)} %collective-permute-done.2) | copy-start | bytes 14745604
  173.7 55.7 %collective-permute-start.3 = (bf16[384,6400]{1,0:T(8,128)(2,1)S(1)}, bf16[384,6400]{1,0:T(8,128)(2,1)S(1)}, u32[]{:S(2)}, u32[]{:S(2)}) collective-permute-start(bf16[384,6400]{1,0:T(8,128)(2,1)S(1)} %collective-permute-done.2), channel_id=1, source_target_pairs={{0,120},{8,0},{16,8},{24,16},{32,24},{40,32},{48,40},{56,48},{64,5... | collective-permute-start | bytes 14745608 | tf_op jit(solution)/shard_map/ppermute | solution.py:10
  229.4 2.2 copy-start.5
  231.5 55.7 %collective-permute-start.4 = (bf16[384,6400]{1,0:T(8,128)(2,1)S(1)}, bf16[384,6400]{1,0:T(8,128)(2,1)S(1)}, u32[]{:S(2)}, u32[]{:S(2)}) collective-permute-start(bf16[384,6400]{1,0:T(8,128)(2,1)S(1)} %collective-permute-done.3), channel_id=1, source_target_pairs={{0,120},{8,0},{16,8},{24,16},{32,24},{40,32},{48,40},{56,48},{64,5... | collective-permute-start | bytes 14745608 | tf_op jit(solution)/shard_map/ppermute | solution.py:10
  287.2 2.2 copy-start.6
  289.4 55.8 %collective-permute-start.5 = (bf16[384,6400]{1,0:T(8,128)(2,1)S(1)}, bf16[384,6400]{1,0:T(8,128)(2,1)}, u32[]{:S(2)}, u32[]{:S(2)}) collective-permute-start(bf16[384,6400]{1,0:T(8,128)(2,1)S(1)} %collective-permute-done.4), channel_id=1, source_target_pairs={{0,120},{8,0},{16,8},{24,16},{32,24},{40,32},{48,40},{56,48},{64,5... | collective-permute-start | bytes 14745608 | tf_op jit(solution)/shard_map/ppermute | solution.py:10
  345.2 56.0 %collective-permute-start.6 = (bf16[384,6400]{1,0:T(8,128)(2,1)}, bf16[384,6400]{1,0:T(8,128)(2,1)}, u32[]{:S(2)}, u32[]{:S(2)}) collective-permute-start(bf16[384,6400]{1,0:T(8,128)(2,1)} %collective-permute-done.5), channel_id=1, source_target_pairs={{0,120},{8,0},{16,8},{24,16},{32,24},{40,32},{48,40},{56,48},{64,5... | collective-permute-start | bytes 14745608 | tf_op jit(solution)/shard_map/ppermute | solution.py:10
  401.1 72.8 %collective-permute-start.7 = (bf16[384,6400]{1,0:T(8,128)(2,1)}, bf16[384,6400]{1,0:T(8,128)(2,1)}, u32[]{:S(2)}, u32[]{:S(2)}) collective-permute-start(bf16[384,6400]{1,0:T(8,128)(2,1)} %collective-permute-done.6), channel_id=1, source_target_pairs={{0,120},{8,0},{16,8},{24,16},{32,24},{40,32},{48,40},{56,48},{64,5... | collective-permute-start | bytes 14745608 | tf_op jit(solution)/shard_map/ppermute | solution.py:10
  478.7 3.3 copy-start.3
  539.6 2.5 copy-start.4
where the time goes:
time: 579 us; the launch traced here: 577 us
  waiting for transfers between devices  303 us (52%)
  matrix products  94.1 us (16%)
  blocking collectives  90.5 us (16%)
  starting transfers between devices  62.9 us (11%)
  local copies, waits for them, and re-layouts  17.8 us (3%)
  other arithmetic  8.08 us (1%)
    ppermute x8, waiting for transfers between devices, from_behind(): return lax.ppermute(value, axis, pairs)  303 us
    ppermute x8, starting transfers between devices, from_behind(): return lax.ppermute(value, axis, pairs)  62.9 us
    all_to_all x1, blocking collectives, copy_for_each(): lax.all_to_all(jnp.broadcast_to(shard[None], (peers, *shard.shape)), axis...  56.5 us
    dot_general x9, matrix products, pair_block(): lax.dot_general(virt_scaled, far_virt, contract, preferred_element_type=j...  39.2 us
    dot_general x9, matrix products, pair_block(): applied = jnp.dot(response, far_pot, preferred_element_type=jnp.float32)  35.6 us
    all_to_all x1, blocking collectives, summed_on_arrival(): lax.all_to_all(parts, axis, split_axis=0, concat_axis=0, tiled=True)  33.9 us
    dot_general x9, matrix products, pair_block(): lax.dot_general(pot_wide, applied, (((0,), (0,)), ((), ())), precision=la...  19.3 us
    dot_general x7, local copies, waits for them, and re-layouts, pair_block(): lax.dot_general(pot_wide, applied, (((0,), (0,)), ((), ())), precision=la...  12.5 us
  transfers between devices with their start and end apart: 8, of which 7 were waited for; matrix products, arithmetic and copies ran while one was open for 17% of the time, Pallas kernels for 0%

commit v1 on v0

v1 whole, which is shorter than its diff:
```python
import functools

import jax
import jax.numpy as jnp
from jax import lax
from jax.experimental import pallas as pl
from jax.experimental.pallas import tpu as pltpu
from jax.sharding import PartitionSpec as P

MESH = pl.DeviceIdType.MESH
NT = (((1,), (1,)), ((), ()))
N_OCC, N_VIRT, N_POT, ROWS = 2048, 4096, 256, 384
N_ORB = N_OCC + N_VIRT
WIDTH = N_ORB + N_POT
TIMES = 8
SLAB = ROWS // TIMES
CHUNK = 16
CHUNKS = SLAB // CHUNK
OWN, A, B, C, D = range(5)
F32, BF16 = jnp.float32, jnp.bfloat16


def kernel(
    occ_ref, virt_ref, pot_ref, energy_ref, tw_ref, out_ref,
    own, far, relay, scaled, resp, applied, factor, tw_all, pot_far, proj,
    load_sem, send_sem, recv_sem, tw_send, tw_recv,
):
    pts, tau = lax.axis_index("pts"), lax.axis_index("tau")
    z_lo, y, core = pts // 8, (pts // 2) % 4, pts % 2
    z_hi, x = tau // 4, tau % 4

    def at(z_lo_=None, y_=None, core_=None, z_hi_=None):
        zl = z_lo if z_lo_ is None else z_lo_
        yy = y if y_ is None else y_
        cc = core if core_ is None else core_
        zh = z_hi if z_hi_ is None else z_hi_
        return (zl * 8 + yy * 2 + cc, zh * 4 + x)

    sibling = at(core_=1 - core)
    z_out = at(z_lo_=1 - z_lo, z_hi_=1 - z_hi)
    z_in = at(z_lo_=1 - z_lo)
    y_down = at(y_=(y + 3) % 4)
    y_up = at(y_=(y + 1) % 4)
    tau_peers = [(pts, (tau + d) % TIMES) for d in range(1, TIMES)]

    first = pl.multiple_of(tau * SLAB, CHUNK)
    parts = ((occ_ref, 0, N_OCC), (virt_ref, N_OCC, N_VIRT), (pot_ref, N_ORB, N_POT))
    loads = []
    for i, (ref, at_col, cols) in enumerate(parts):
        loads.append(pltpu.make_async_copy(
            ref.at[pl.ds(first, SLAB)], far.at[OWN, :, pl.ds(at_col, cols)], load_sem.at[i]))
    for i, (ref, at_col, cols) in enumerate(parts):
        loads.append(pltpu.make_async_copy(
            ref, own.at[pl.ds(0, ROWS), pl.ds(at_col, cols)], load_sem.at[3 + i]))
    for load in loads:
        load.start()

    barrier = pltpu.get_barrier_semaphore()
    greeted = [sibling, z_out, z_in, y_down, y_up] + tau_peers
    for peer in greeted:
        pl.semaphore_signal(barrier, 1, device_id=peer, device_id_type=MESH)
    tw_all[tau] = tw_ref[...]
    pl.semaphore_wait(barrier, len(greeted))

    count = iter(range(64))
    sent = []

    def send(src, dst, peer):
        i = next(count)
        copy = pltpu.make_async_remote_copy(
            src_ref=src, dst_ref=dst, send_sem=send_sem.at[i], recv_sem=recv_sem.at[i],
            device_id=peer, device_id_type=MESH)
        copy.start()
        sent.append(copy)
        return copy

    tw_copies = []
    for i, peer in enumerate(tau_peers):
        copy = pltpu.make_async_remote_copy(
            src_ref=tw_ref, dst_ref=tw_all.at[tau], send_sem=tw_send.at[i], recv_sem=tw_recv.at[i],
            device_id=peer, device_id_type=MESH)
        copy.start()
        tw_copies.append(copy)

    def rows_of(k):
        return pl.ds(k * CHUNK, CHUNK)

    for load in loads[:3]:
        load.wait()
    got_b = [send(far.at[OWN, rows_of(k)], far.at[B, rows_of(k)], y_down) for k in range(CHUNKS)]
    for load in loads[3:]:
        load.wait()
    out_first = ((1 - z_hi) * 4 + x) * SLAB
    got_a = {}
    for k in (1, 2, 0):
        rows = pl.ds(pl.multiple_of(out_first + k * CHUNK, CHUNK), CHUNK)
        got_a[k] = send(own.at[rows], far.at[A, rows_of(k)], z_out)
    got_own = send(own.at[pl.ds(0, ROWS)], own.at[pl.ds(ROWS, ROWS)], sibling)

    for copy in tw_copies:
        copy.wait()
    for t in range(TIMES):
        factor[t] = jnp.exp(tw_all[t, 8:9, 0:1] * energy_ref[...])

    def scale(slot, k, t_first, t_count):
        def one(i, carry):
            t = t_first + i
            wide = far[slot, rows_of(k), pl.ds(0, N_ORB)].astype(F32) * factor[t]
            scaled[pl.ds(pl.multiple_of(i * SLAB + k * CHUNK, CHUNK), CHUNK)] = wide.astype(BF16)
            return carry
        lax.fori_loop(0, t_count, one, 0)

    def tile(n, t_count):
        lines = t_count * SLAB
        n0 = pl.multiple_of(n * 256, 256)
        g_occ = lax.dot_general(
            scaled[:lines, :N_OCC], own[pl.ds(n0, 256), :N_OCC], NT, preferred_element_type=F32)
        g_virt = lax.dot_general(
            scaled[:lines, N_OCC:], own[pl.ds(n0, 256), N_OCC:N_ORB], NT, preferred_element_type=F32)
        resp[:lines, pl.ds(n0, 256)] = (-(g_occ * g_virt)).astype(BF16)

    def apply(slot, t_first, t_count):
        lines = t_count * SLAB
        part = jnp.dot(resp[:lines], own[:, N_ORB:], preferred_element_type=F32)
        applied[pl.ds(t_first, t_count), slot * SLAB:(slot + 1) * SLAB, :] = part.reshape(
            t_count, SLAB, N_POT)

    for k in range(CHUNKS):
        scale(OWN, k, 0, TIMES)
    tile(0, TIMES)
    got_own.wait_recv()
    tile(1, TIMES)
    got_c, got_relay, got_d = [], {}, {}

    def pass_c(k):
        got_b[k].wait_recv()
        got_c.append(send(far.at[B, rows_of(k)], far.at[C, rows_of(k)], z_in))

    def pass_up(k):
        got_a[k].wait_recv()
        slot = jnp.where((y + 2) % 4 < 2, OWN, A)
        got_relay[k] = send(far.at[slot, rows_of(k)], relay.at[k - 1], y_up)

    def pass_d(k):
        got_relay[k].wait_recv()
        got_d[k] = send(relay.at[k - 1], far.at[D, rows_of(k)], y_up)

    pass_c(0)
    pass_up(1)
    tile(2, TIMES)
    apply(OWN, 0, TIMES)
    pass_c(1)
    pass_up(2)
    half = TIMES // 2
    t_mine, t_other = z_lo * half, (1 - z_lo) * half
    scale(A, 1, t_mine, half)
    scale(A, 2, t_mine, half)
    got_a[0].wait_recv()
    scale(A, 0, t_mine, half)
    for n in range(3):
        tile(n, half)
    apply(A, t_mine, half)
    applied[pl.ds(t_other, half), A * SLAB:(A + 1) * SLAB, :] = jnp.zeros((half, SLAB, N_POT), F32)
    pass_c(2)
    pass_d(1)
    got_c[0].wait_recv()
    slot = jnp.where((y + 3) % 4 < 2, B, C)
    got_d[0] = send(far.at[slot, rows_of(0)], far.at[D, rows_of(0)], y_down)
    for k in range(CHUNKS):
        scale(B, k, 0, TIMES)
    tile(0, TIMES)
    pass_d(2)
    tile(1, TIMES)
    tile(2, TIMES)
    apply(B, 0, TIMES)
    for k in range(CHUNKS):
        if k:
            got_c[k].wait_recv()
        scale(C, k, 0, TIMES)
    for n in range(3):
        tile(n, TIMES)
    apply(C, 0, TIMES)
    for k in range(CHUNKS):
        got_d[k].wait_recv()
        scale(D, k, 0, TIMES)
    for n in range(3):
        tile(n, TIMES)
    apply(D, 0, TIMES)

    pot_far[0:SLAB] = far[OWN, :, N_ORB:] * jnp.asarray(0.5, BF16)
    for slot in (A, B, C, D):
        pot_far[slot * SLAB:(slot + 1) * SLAB] = far[slot, :, N_ORB:]
    used = 5 * SLAB
    pot_far[used:] = jnp.zeros((N_POT - used, N_POT), BF16)
    pot_t = pot_far[...].T
    applied[:, used:, :] = jnp.zeros((TIMES, N_POT - used, N_POT), F32)

    def project(t, carry):
        whole = applied[t]
        high = whole.astype(BF16)
        low = (whole - high.astype(F32)).astype(BF16)
        both = jnp.dot(pot_t, high, preferred_element_type=F32) + jnp.dot(
            pot_t, low, preferred_element_type=F32)
        proj[t, 0:128] = both[:128, :128]
        proj[t, 128:256] = both[:128, 128:] + both[128:, :128].T
        proj[t, 256:384] = both[128:, 128:]
        return carry

    lax.fori_loop(0, TIMES, project, 0)

    def combine(w, carry):
        total = tw_all[0, pl.ds(w, 1), :] * proj[0]
        for t in range(1, TIMES):
            total = total + tw_all[t, pl.ds(w, 1), :] * proj[t]
        out_ref[w] = total
        return carry

    lax.fori_loop(0, TIMES, combine, 0)
    for copy in sent:
        copy.wait_send()


def body(occ, virt, pot, occ_energy, virt_energy, times, weights):
    energy = jnp.concatenate([occ_energy, -virt_energy])[None, :]
    tw = jnp.concatenate(
        [jnp.broadcast_to(weights, (TIMES, 128)), jnp.broadcast_to(times[None, :], (8, 128))], axis=0)
    anywhere, vmem = pl.BlockSpec(memory_space=pl.ANY), pl.BlockSpec(memory_space=pltpu.VMEM)
    sums = pl.pallas_call(
        kernel,
        out_shape=jax.ShapeDtypeStruct((TIMES, 384, 128), F32),
        in_specs=[anywhere] * 3 + [vmem] * 2,
        out_specs=vmem,
        scratch_shapes=[
            pltpu.VMEM((2 * ROWS, WIDTH), BF16),
            pltpu.VMEM((5, SLAB, WIDTH), BF16),
            pltpu.VMEM((2, CHUNK, WIDTH), BF16),
            pltpu.VMEM((TIMES * SLAB, N_ORB), BF16),
            pltpu.VMEM((TIMES * SLAB, 2 * ROWS), BF16),
            pltpu.VMEM((TIMES, N_POT, N_POT), F32),
            pltpu.VMEM((TIMES, 1, N_ORB), F32),
            pltpu.VMEM((TIMES, 16, 128), F32),
            pltpu.VMEM((N_POT, N_POT), BF16),
            pltpu.VMEM((TIMES, 384, 128), F32),
            pltpu.SemaphoreType.DMA((6,)),
            pltpu.SemaphoreType.DMA((24,)),
            pltpu.SemaphoreType.DMA((24,)),
            pltpu.SemaphoreType.DMA((7,)),
            pltpu.SemaphoreType.DMA((7,)),
        ],
        compiler_params=pltpu.CompilerParams(
            collective_id=0, has_side_effects=True, vmem_limit_bytes=48 * 2**20),
    )(occ, virt, pot, energy, tw)
    mine = lax.psum_scatter(sums, "tau", scatter_dimension=0, tiled=True)
    mine = lax.psum(mine, "pts")[0]
    low, mid, high = mine[:128], mine[128:256], mine[256:]
    top = jnp.concatenate([low + low.T, mid], axis=1)
    bottom = jnp.concatenate([mid.T, high + high.T], axis=1)
    return jnp.concatenate([top, bottom], axis=0)[None]


def solution(mesh):
    return jax.shard_map(
        body,
        mesh=mesh,
        in_specs=(P("pts", None), P("pts", None), P("pts", None), P(), P(), P("tau"), P(None, "tau")),
        out_specs=P("tau", None, None),
        check_vma=False,
    )
```

time: 579 us -> 258 us (0.45)
  waiting for transfers between devices: 303 us -> 184 us
  matrix products: 94.1 us -> 0 us
  blocking collectives: 90.5 us -> 0 us
  starting transfers between devices: 62.9 us -> 0.04 us
  Pallas kernels: 0 us -> 50.9 us
  local copies, waits for them, and re-layouts: 17.8 us -> 4.26 us
  between operations: 0.94 us -> 14.1 us
    ppermute x8 -> x0, waiting for transfers between devices: 303 us -> none  [from_behind(): return lax.ppermute(value, axis, pairs)]
    psum x0 -> x1, waiting for transfers between devices: none -> 113 us  [body(): mine = lax.psum(mine, 'pts')[0]]
    dot_general x27 -> x0, matrix products: 94.1 us -> none  [the longest x9 39.2 us: pair_block(): lax.dot_general(virt_scaled, far_virt, contract, preferred_element_type=j...]
    all_to_all x2 -> x0, blocking collectives: 90.5 us -> none  [the longest x1 56.5 us: copy_for_each(): lax.all_to_all(jnp.broadcast_to(shard[None], (peers, *shard.shape)), axis...]
    reduce_scatter x0 -> x1, waiting for transfers between devices: none -> 71.3 us  [body(): mine = lax.psum_scatter(sums, 'tau', scatter_dimension=0, tiled=True)]
    ppermute x8 -> x0, starting transfers between devices: 62.9 us -> none  [from_behind(): return lax.ppermute(value, axis, pairs)]
    pallas_call x0 -> x1, Pallas kernels: none -> 50.9 us  [body(): pl.pallas_call(kernel, out_shape=jax.ShapeDtypeStruct((TIMES, 384, 128),...]
    dot_general x7 -> x0, local copies, waits for them, and re-layouts: 12.5 us -> none  [pair_block(): lax.dot_general(pot_wide, applied, (((0,), (0,)), ((), ())), precision=la...]
  transfers between devices with their start and end apart: 8 -> 2, of which waited for: 7 -> 2; matrix products, arithmetic and copies ran while one was open for 17% -> 0% of each run, Pallas kernels for 0% -> 0%
where the time goes in v1:
time: 258 us; the launch traced here: 257 us
  waiting for transfers between devices  184 us (71%)
  Pallas kernels  50.9 us (20%)
  between operations  14.1 us (5%)
  local copies, waits for them, and re-layouts  4.26 us (2%)
  other arithmetic  3.04 us (1%)
    psum x1, waiting for transfers between devices, body(): mine = lax.psum(mine, 'pts')[0]  113 us
    reduce_scatter x1, waiting for transfers between devices, body(): mine = lax.psum_scatter(sums, 'tau', scatter_dimension=0, tiled=True)  71.3 us
    pallas_call x1, Pallas kernels, body(): pl.pallas_call(kernel, out_shape=jax.ShapeDtypeStruct((TIMES, 384, 128),...  50.9 us
  transfers between devices with their start and end apart: 2, of which 2 were waited for; matrix products, arithmetic and copies ran while one was open for 0% of the time, Pallas kernels for 0%

profile of v1, /device:TPU:1, one launch (start us, length us, event | category | flops | bytes accessed | tf_op | source)
XLA Modules:
  0.0 256.7 jit_solution(12178767949016925741)
XLA Ops:
  6.5 0.0 reduce-scatter.2.cloned.1.call-start
  7.2 0.7 neg.3
  7.9 0.7 concatenate.18
  8.6 0.7 pad_maximum_fusion
  9.3 0.1 concatenate.19.tw_ref
  9.3 0.0 copy-start
  9.3 1.4 copy-done
  10.7 0.0 copy-start.1
  10.8 0.9 copy-done.1
  11.7 50.9 %shard_map.73 = f32[8,384,128]{2,1,0:T(8,128)} custom-call(bf16[384,2048]{1,0:T(8,128)(2,1)S(1)} %copy-done, bf16[384,4096]{1,0:T(8,128)(2,1)} %virt_ref.1, bf16[384,256]{1,0:T(8,128)(2,1)S(1)} %copy-done.1, f32[1,6144]{1,0:T(1,128)S(1)} %bitcast.23, f32[16,128]{1,0:T(8,128)S(1)} %concatenate.19.tw_ref), custom_call_target="tpu_custom_call" | custom-call | tf_op jit(solution)/shard_map/pallas_call | solution.py:228
  62.6 0.0 reduce-scatter.2.cloned.1.call-update
  62.6 0.0 all-reduce.3.cloned.1.call-start
  62.6 71.3 %reduce-scatter.2.cloned.1.call-done = f32[1,384,128]{2,1,0:T(8,128)} async-done(((f32[8,384,128]{2,1,0:T(8,128)}), f32[1,384,128]{2,1,0:T(8,128)}) %reduce-scatter.2.cloned.1.call-update) | async-done | bytes 196624 | tf_op jit(solution)/shard_map/reduce_scatter | solution.py:253
  134.0 0.0 all-reduce.3.cloned.1.call-update
  134.0 113.0 %all-reduce.3.cloned.1.call-done = f32[1,384,128]{2,1,0:T(8,128)} async-done(((f32[1,384,128]{2,1,0:T(8,128)}), f32[1,384,128]{2,1,0:T(8,128)}) %all-reduce.3.cloned.1.call-update) | async-done | bytes 196624 | tf_op jit(solution)/shard_map/psum | solution.py:254
  247.0 0.9 fusion
  247.9 0.1 copy.12
  248.0 0.1 copy.11
  248.1 0.1 copy.10
  248.2 0.9 bitcast_add_fusion
  249.1 0.7 maximum_bitcast_fusion
Async XLA Ops:
  6.5 127.4 %reduce-scatter.2.cloned.1.call-start = ((), (), s32[]{:S(2)}) async-start(), calls=%async_computation.1 | async-start | bytes 1769472 | tf_op jit(solution)/shard_map/reduce_scatter | solution.py:253
  9.3 1.4 copy-start
  10.7 0.9 copy-start.1
  62.6 184.4 %all-reduce.3.cloned.1.call-start = ((), (), s32[]{:S(2)}) async-start(), calls=%async_computation.2 | async-start | bytes 393216 | tf_op jit(solution)/shard_map/psum | solution.py:254
Sparse Core Ops, SparseCore 0:
  62.7 71.2 reduce-scatter.1
  136.4 110.5 all-reduce.2

commit v2 on v1

--- a/solution.py
+++ b/solution.py
@@ -21,9 +21,11 @@
 
 
 def kernel(
-    occ_ref, virt_ref, pot_ref, energy_ref, tw_ref, out_ref,
-    own, far, relay, scaled, resp, applied, factor, tw_all, pot_far, proj,
+    occ_ref, virt_ref, pot_ref, occ_e_ref, virt_e_ref, times_ref, weights_ref, out_ref,
+    own, far, relay, scaled, resp, applied, factor, tw_mine, tw_all, pot_far, proj,
+    sums, from_core, arrive1, arrive2, arrive3, left1, left2, final, whole_out,
     load_sem, send_sem, recv_sem, tw_send, tw_recv,
+    core_sem, ring_send, ring_recv, all_send, all_recv,
 ):
     pts, tau = lax.axis_index("pts"), lax.axis_index("tau")
     z_lo, y, core = pts // 8, (pts // 2) % 4, pts % 2
@@ -56,10 +58,13 @@
         load.start()
 
     barrier = pltpu.get_barrier_semaphore()
-    greeted = [sibling, z_out, z_in, y_down, y_up] + tau_peers
+    pts_peers = [((pts + d) % 16, tau) for d in range(1, 16)]
+    greeted = [z_out] + pts_peers + tau_peers
     for peer in greeted:
         pl.semaphore_signal(barrier, 1, device_id=peer, device_id_type=MESH)
-    tw_all[tau] = tw_ref[...]
+    tw_mine[0:8] = jnp.broadcast_to(weights_ref[...], (8, 128))
+    tw_mine[8:16] = jnp.broadcast_to(times_ref[...], (8, 128))
+    tw_all[tau] = tw_mine[...]
     pl.semaphore_wait(barrier, len(greeted))
 
     count = iter(range(64))
@@ -77,7 +82,7 @@
     tw_copies = []
     for i, peer in enumerate(tau_peers):
         copy = pltpu.make_async_remote_copy(
-            src_ref=tw_ref, dst_ref=tw_all.at[tau], send_sem=tw_send.at[i], recv_sem=tw_recv.at[i],
+            src_ref=tw_mine, dst_ref=tw_all.at[tau], send_sem=tw_send.at[i], recv_sem=tw_recv.at[i],
             device_id=peer, device_id_type=MESH)
         copy.start()
         tw_copies.append(copy)
@@ -98,9 +103,11 @@
     got_own = send(own.at[pl.ds(0, ROWS)], own.at[pl.ds(ROWS, ROWS)], sibling)
 
     for copy in tw_copies:
-        copy.wait()
+        copy.wait_recv()
     for t in range(TIMES):
-        factor[t] = jnp.exp(tw_all[t, 8:9, 0:1] * energy_ref[...])
+        moment = tw_all[t, 8:9, 0:1]
+        factor[t, :, :N_OCC] = jnp.exp(moment * occ_e_ref[...])
+        factor[t, :, N_OCC:] = jnp.exp(-moment * virt_e_ref[...])
 
     def scale(slot, k, t_first, t_count):
         def one(i, carry):
@@ -209,26 +216,94 @@
     lax.fori_loop(0, TIMES, project, 0)
 
     def combine(w, carry):
-        total = tw_all[0, pl.ds(w, 1), :] * proj[0]
-        for t in range(1, TIMES):
-            total = total + tw_all[t, pl.ds(w, 1), :] * proj[t]
-        out_ref[w] = total
+        w_zh, w_x = w // 4, w % 4
+        weight = [tw_all[t, pl.ds(w, 1), :] for t in range(TIMES)]
+        for h in range(2):
+            for a in range(3):
+                for zl in range(2):
+                    for yy in range(4):
+                        rows = pl.ds(((h * 3 + a) * 8 + zl * 4 + yy) * 8, 8)
+                        total = weight[0] * proj[0, rows]
+                        for t in range(1, TIMES):
+                            total = total + weight[t] * proj[t, rows]
+                        zz = w_zh * 2 + zl
+                        place = ((w_x, yy, zz), (yy, zz, w_x), (zz, w_x, yy))[a]
+                        sums[h, a, place[0], place[1], place[2]] = total
         return carry
 
     lax.fori_loop(0, TIMES, combine, 0)
-    for copy in sent:
+
+    swap = pltpu.make_async_remote_copy(
+        src_ref=sums.at[1 - core], dst_ref=from_core, send_sem=core_sem.at[0], recv_sem=core_sem.at[1],
+        device_id=sibling, device_id_type=MESH)
+    swap.start()
+    swap.wait_recv()
+    z = z_hi * 2 + z_lo
+    place = (x, y, z)
+
+    def along(axis, index):
+        if axis == 0:
+            return (pts, z_hi * 4 + index)
+        if axis == 1:
+            return at(y_=index)
+        return at(z_lo_=index % 2, z_hi_=index // 2)
+
+    for a in range(3):
+        from_core[a] = from_core[a] + sums[core, a]
+    held = from_core
+    copies = []
+    for stage, (arrive, left) in enumerate(((arrive1, left1), (arrive2, left2), (arrive3, final))):
+        wave = []
+        for a in range(3):
+            axis = (a + stage) % 3
+            for d in (2, 1, 3):
+                index = (place[axis] + d) % 4
+                i = (stage * 3 + a) * 3 + d - 1
+                copy = pltpu.make_async_remote_copy(
+                    src_ref=held.at[a, index], dst_ref=arrive.at[a, d - 1],
+                    send_sem=ring_send.at[i], recv_sem=ring_recv.at[i],
+                    device_id=along(axis, index), device_id_type=MESH)
+                copy.start()
+                wave.append(copy)
+        copies += wave
+        for a in range(3):
+            for copy in wave[3 * a:3 * a + 3]:
+                copy.wait_recv()
+            left[a] = held[a, place[(a + stage) % 3]] + arrive[a, 0] + arrive[a, 1] + arrive[a, 2]
+        held = left
+
+    wave = []
+    for i, peer in enumerate(pts_peers):
+        copy = pltpu.make_async_remote_copy(
+            src_ref=final, dst_ref=whole_out.at[pts], send_sem=all_send.at[i], recv_sem=all_recv.at[i],
+            device_id=peer, device_id_type=MESH)
+        copy.start()
+        wave.append(copy)
+    whole_out[pts] = final[...]
+    for copy in wave:
+        copy.wait_recv()
+    rows = []
+    for h in range(2):
+        for a in range(3):
+            for zl in range(2):
+                for yy in range(4):
+                    rows.append(whole_out[zl * 8 + yy * 2 + h, a])
+    low, mid, high = [jnp.concatenate(rows[16 * b:16 * b + 16], axis=0) for b in range(3)]
+    out_ref[0, :128, :128] = low + low.T
+    out_ref[0, :128, 128:] = mid
+    out_ref[0, 128:, :128] = mid.T
+    out_ref[0, 128:, 128:] = high + high.T
+    swap.wait_send()
+    for copy in sent + copies + wave + tw_copies:
         copy.wait_send()
 
 
 def body(occ, virt, pot, occ_energy, virt_energy, times, weights):
-    energy = jnp.concatenate([occ_energy, -virt_energy])[None, :]
-    tw = jnp.concatenate(
-        [jnp.broadcast_to(weights, (TIMES, 128)), jnp.broadcast_to(times[None, :], (8, 128))], axis=0)
     anywhere, vmem = pl.BlockSpec(memory_space=pl.ANY), pl.BlockSpec(memory_space=pltpu.VMEM)
-    sums = pl.pallas_call(
+    return pl.pallas_call(
         kernel,
-        out_shape=jax.ShapeDtypeStruct((TIMES, 384, 128), F32),
-        in_specs=[anywhere] * 3 + [vmem] * 2,
+        out_shape=jax.ShapeDtypeStruct((1, N_POT, N_POT), F32),
+        in_specs=[anywhere] * 3 + [vmem] * 4,
         out_specs=vmem,
         scratch_shapes=[
             pltpu.VMEM((2 * ROWS, WIDTH), BF16),
@@ -238,24 +313,33 @@
             pltpu.VMEM((TIMES * SLAB, 2 * ROWS), BF16),
             pltpu.VMEM((TIMES, N_POT, N_POT), F32),
             pltpu.VMEM((TIMES, 1, N_ORB), F32),
+            pltpu.VMEM((16, 128), F32),
             pltpu.VMEM((TIMES, 16, 128), F32),
             pltpu.VMEM((N_POT, N_POT), BF16),
             pltpu.VMEM((TIMES, 384, 128), F32),
+            pltpu.VMEM((2, 3, 4, 4, 4, 8, 128), F32),
+            pltpu.VMEM((3, 4, 4, 4, 8, 128), F32),
+            pltpu.VMEM((3, 3, 4, 4, 8, 128), F32),
+            pltpu.VMEM((3, 3, 4, 8, 128), F32),
+            pltpu.VMEM((3, 3, 8, 128), F32),
+            pltpu.VMEM((3, 4, 4, 8, 128), F32),
+            pltpu.VMEM((3, 4, 8, 128), F32),
+            pltpu.VMEM((3, 8, 128), F32),
+            pltpu.VMEM((16, 3, 8, 128), F32),
             pltpu.SemaphoreType.DMA((6,)),
             pltpu.SemaphoreType.DMA((24,)),
             pltpu.SemaphoreType.DMA((24,)),
             pltpu.SemaphoreType.DMA((7,)),
             pltpu.SemaphoreType.DMA((7,)),
+            pltpu.SemaphoreType.DMA((2,)),
+            pltpu.SemaphoreType.DMA((27,)),
+            pltpu.SemaphoreType.DMA((27,)),
+            pltpu.SemaphoreType.DMA((15,)),
+            pltpu.SemaphoreType.DMA((15,)),
         ],
         compiler_params=pltpu.CompilerParams(
-            collective_id=0, has_side_effects=True, vmem_limit_bytes=48 * 2**20),
-    )(occ, virt, pot, energy, tw)
-    mine = lax.psum_scatter(sums, "tau", scatter_dimension=0, tiled=True)
-    mine = lax.psum(mine, "pts")[0]
-    low, mid, high = mine[:128], mine[128:256], mine[256:]
-    top = jnp.concatenate([low + low.T, mid], axis=1)
-    bottom = jnp.concatenate([mid.T, high + high.T], axis=1)
-    return jnp.concatenate([top, bottom], axis=0)[None]
+            collective_id=0, has_side_effects=True, vmem_limit_bytes=60 * 2**20),
+    )(occ, virt, pot, occ_energy[None, :], virt_energy[None, :], times[None, :], weights)
 
 
 def solution(mesh):

time: 258 us -> 75.9 us (0.29)
  waiting for transfers between devices: 184 us -> 0 us
  Pallas kernels: 50.9 us -> 72 us
  between operations: 14.1 us -> 0.66 us
  other arithmetic: 3.04 us -> 0 us
    psum x1 -> x0, waiting for transfers between devices: 113 us -> none  [body(): mine = lax.psum(mine, 'pts')[0]]
    reduce_scatter x1 -> x0, waiting for transfers between devices: 71.3 us -> none  [body(): mine = lax.psum_scatter(sums, 'tau', scatter_dimension=0, tiled=True)]
    pallas_call x1, Pallas kernels: 50.9 us -> 72 us  [body(): pl.pallas_call(kernel, out_shape=jax.ShapeDtypeStruct((1, N_POT, N_POT),...]
  transfers between devices with their start and end apart: 2 -> 0, of which waited for: 2 -> 0; matrix products, arithmetic and copies ran while one was open for 0% -> 0% of each run, Pallas kernels for 0% -> 0%
where the time goes in v2:
time: 75.9 us; the launch traced here: 75.7 us
  Pallas kernels  72 us (95%)
  local copies, waits for them, and re-layouts  2.99 us (4%)
    pallas_call x1, Pallas kernels, body(): pl.pallas_call(kernel, out_shape=jax.ShapeDtypeStruct((1, N_POT, N_POT),...  72 us
    unnamed x2, local copies, waits for them, and re-layouts  2.99 us

profile of v2, /device:TPU:1, one launch (start us, length us, event | category | flops | bytes accessed | tf_op | source)
XLA Modules:
  0.0 75.7 jit_solution(13036629860856181349)
XLA Ops:
  0.7 1.3 %copy.8.weights_ref = f32[8,1]{1,0:T(8,128)} copy(f32[8,1]{0,1:T(1,128)} %param.13) | data formatting | bytes 64 | tf_op args[6]
  2.0 72.0 %shard_map.73 = f32[1,256,256]{2,1,0:T(8,128)} custom-call(bf16[384,2048]{1,0:T(8,128)(2,1)} %occ_ref.1, bf16[384,4096]{1,0:T(8,128)(2,1)} %virt_ref.1, bf16[384,256]{1,0:T(8,128)(2,1)} %pot_ref.1, f32[1,2048]{1,0:T(1,128)} %bitcast.5, f32[1,4096]{1,0:T(1,128)} %bitcast.4, f32[1,1]{1,0:T(1,128)} %bitcast.3.times_ref, f32[8,1]{1,0:T(8,128)} %copy.8.weights_ref), custom_call_target="tpu_custom_call" | custom-call | tf_op jit(solution)/shard_map/pallas_call | solution.py:303
  74.0 1.7 %copy.11 = f32[1,256,256]{2,1,0:T(8,128)} copy(f32[1,256,256]{2,1,0:T(8,128)} %shard_map.73) | data formatting | bytes 524288

commit v3 on v2

v3 whole, which is shorter than its diff:
```python
import functools

import jax
import jax.numpy as jnp
from jax import lax
from jax.experimental import pallas as pl
from jax.experimental.pallas import tpu as pltpu
from jax.sharding import PartitionSpec as P

MESH = pl.DeviceIdType.MESH
NT = (((1,), (1,)), ((), ()))
N_OCC, N_VIRT, N_POT, ROWS = 2048, 4096, 256, 384
N_ORB = N_OCC + N_VIRT
WIDTH = N_ORB + N_POT
TIMES = 8
SLAB = ROWS // TIMES
CHUNK = 16
CHUNKS = SLAB // CHUNK
OWN, B, C, D, A = range(5)
F32, BF16 = jnp.float32, jnp.bfloat16


def kernel(
    occ_ref, virt_ref, pot_ref, occ_e_ref, virt_e_ref, times_ref, weights_ref, out_ref,
    own, far, relay, scaled, resp, applied, factor, tw_all, pot_far, proj,
    sums, from_core, arrive1, arrive2, arrive3, left1, left2, final, quad, whole_out,
    load_sem, send_sem, recv_sem, tw_send, tw_recv,
    core_sem, ring_send, ring_recv, all_send, all_recv,
):
    pts, tau = lax.axis_index("pts"), lax.axis_index("tau")
    z_lo, y, core = pts // 8, (pts // 2) % 4, pts % 2
    z_hi, x = tau // 4, tau % 4

    def at(z_lo_=None, y_=None, core_=None, z_hi_=None):
        zl = z_lo if z_lo_ is None else z_lo_
        yy = y if y_ is None else y_
        cc = core if core_ is None else core_
        zh = z_hi if z_hi_ is None else z_hi_
        return (zl * 8 + yy * 2 + cc, zh * 4 + x)

    sibling = at(core_=1 - core)
    z_out = at(z_lo_=1 - z_lo, z_hi_=1 - z_hi)
    z_in = at(z_lo_=1 - z_lo)
    y_down = at(y_=(y + 3) % 4)
    y_up = at(y_=(y + 1) % 4)
    z_in_sibling = at(z_lo_=1 - z_lo, core_=1 - core)
    z_far = at(z_hi_=1 - z_hi)
    x_peers = [(pts, z_hi * 4 + (x + d) % 4) for d in range(1, 4)]
    y_across = at(y_=(y + 2) % 4)

    first = pl.multiple_of(tau * SLAB, CHUNK)
    parts = ((occ_ref, 0, N_OCC), (virt_ref, N_OCC, N_VIRT), (pot_ref, N_ORB, N_POT))
    loads = []
    for i, (ref, at_col, cols) in enumerate(parts):
        loads.append(pltpu.make_async_copy(
            ref.at[pl.ds(first, SLAB)], far.at[OWN, :, pl.ds(at_col, cols)], load_sem.at[i]))
    for i, (ref, at_col, cols) in enumerate(parts):
        loads.append(pltpu.make_async_copy(
            ref, own.at[pl.ds(0, ROWS), pl.ds(at_col, cols)], load_sem.at[3 + i]))
    for load in loads:
        load.start()

    barrier = pltpu.get_barrier_semaphore()
    greeted = [sibling, z_in, z_in_sibling, z_out, z_far, y_down, y_up, y_across] + x_peers
    for peer in greeted:
        pl.semaphore_signal(barrier, 1, device_id=peer, device_id_type=MESH)
    here = x * 2 + z_hi
    for w in range(TIMES):
        tw_all[here, w:w + 1] = jnp.full((1, 128), weights_ref[0, w], F32)
    tw_all[here, 8:16] = jnp.full((8, 128), times_ref[0], F32)
    pl.semaphore_wait(barrier, len(greeted))

    count = iter(range(64))
    sent = []

    def to(src, dst, peer):
        i = next(count)
        copy = pltpu.make_async_remote_copy(
            src_ref=src, dst_ref=dst, send_sem=send_sem.at[i], recv_sem=recv_sem.at[i],
            device_id=peer, device_id_type=MESH)
        sent.append(copy)
        return copy

    def send(src, dst, peer):
        copy = to(src, dst, peer)
        copy.start()
        return copy

    def send_tw(i, first, tiles, peer):
        copy = pltpu.make_async_remote_copy(
            src_ref=tw_all.at[pl.ds(first, tiles)], dst_ref=tw_all.at[pl.ds(first, tiles)],
            send_sem=tw_send.at[i], recv_sem=tw_recv.at[i], device_id=peer, device_id_type=MESH)
        copy.start()
        return copy

    tw_copies = [send_tw(0, here, 1, z_far)]

    def rows_of(k):
        return pl.ds(k * CHUNK, CHUNK)

    for load in loads[:3]:
        load.wait()
    got_b = [send(far.at[OWN, rows_of(k)], far.at[B, rows_of(k)], y_down) for k in range(CHUNKS)]
    for load in loads[3:]:
        load.wait()
    out_first = ((1 - z_hi) * 4 + x) * SLAB

    def own_rows(start, k):
        return own.at[pl.ds(pl.multiple_of(start + k * CHUNK, CHUNK), CHUNK)]

    got_a = {
        2: send(own_rows(first, 2), far.at[A, rows_of(2)], z_in),
        1: send(own_rows(out_first, 1), far.at[A, rows_of(1)], z_out),
        0: send(own_rows(out_first, 0), far.at[A, rows_of(0)], z_out),
    }
    got_own = send(own.at[pl.ds(0, ROWS)], own.at[pl.ds(ROWS, ROWS)], sibling)

    tw_copies[0].wait_recv()
    tw_copies += [send_tw(1 + i, x * 2, 2, peer) for i, peer in enumerate(x_peers)]
    for copy in tw_copies[1:]:
        copy.wait_recv()

    def tw_at(t):
        return (t % 4) * 2 + t // 4

    for t in range(TIMES):
        moment = tw_all[tw_at(t), 8:9, 0:1]
        factor[t, :, :N_OCC] = jnp.exp(moment * occ_e_ref[...])
        factor[t, :, N_OCC:] = jnp.exp(-moment * virt_e_ref[...])

    def scale(slot, t_first, t_count):
        def one(i, carry):
            rows = pl.ds(pl.multiple_of((i % CHUNKS) * CHUNK, CHUNK), CHUNK)
            wide = far[slot, rows, pl.ds(0, N_ORB)].astype(F32) * factor[t_first + i // CHUNKS]
            scaled[pl.ds(pl.multiple_of(i * CHUNK, CHUNK), CHUNK)] = wide.astype(BF16)
            return carry
        lax.fori_loop(0, t_count * CHUNKS, one, 0)

    def tile(n, t_count):
        lines = t_count * SLAB
        n0 = pl.multiple_of(n * 256, 256)
        g_occ = lax.dot_general(
            scaled[:lines, :N_OCC], own[pl.ds(n0, 256), :N_OCC], NT, preferred_element_type=F32)
        g_virt = lax.dot_general(
            scaled[:lines, N_OCC:], own[pl.ds(n0, 256), N_OCC:N_ORB], NT, preferred_element_type=F32)
        resp[:lines, pl.ds(n0, 256)] = (-(g_occ * g_virt)).astype(BF16)

    def apply(slot, t_first, t_count):
        lines = t_count * SLAB
        part = jnp.dot(resp[:lines], own[:, N_ORB:], preferred_element_type=F32)
        rows = pl.ds(pl.multiple_of(slot * SLAB, CHUNK), SLAB)
        applied[pl.ds(t_first, t_count), rows, :] = part.reshape(t_count, SLAB, N_POT)

    got_c = [to(far.at[B, rows_of(k)], far.at[C, rows_of(k)], z_in) for k in range(CHUNKS)]
    up_slot = jnp.where((y + 2) % 4 < 2, OWN, A)
    got_relay = to(far.at[up_slot, rows_of(2)], relay, y_up)
    down_slot = jnp.where((y + 3) % 4 < 2, B, C)
    got_d = [to(far.at[down_slot, rows_of(k)], far.at[D, rows_of(k)], y_down) for k in range(2)]
    got_d.append(to(relay, far.at[D, rows_of(2)], y_up))

    def pass_c(k):
        got_b[k].wait_recv()
        got_c[k].start()

    def pass_d(k):
        got_c[k].wait_recv()
        got_d[k].start()

    pass_c(0)
    got_a[2].wait_recv()
    got_relay.start()
    half = TIMES // 2
    t_mine, t_other = z_lo * half, (1 - z_lo) * half

    def half_tile(n, carry):
        @pl.when(n == 1)
        def _():
            got_relay.wait_recv()
            got_d[2].start()
            pass_d(0)
        tile(n, half)
        return carry

    def step(n, carry):
        slot, column = n // 3, n % 3

        @pl.when(n == 1)
        def _():
            got_own.wait_recv()

        @pl.when(n == 3)
        def _():
            pass_c(1)
            got_a[1].wait_recv()
            got_a[0].wait_recv()
            scale(A, t_mine, half)
            lax.fori_loop(0, 3, half_tile, 0)
            apply(A, t_mine, half)
            applied[pl.ds(t_other, half), A * SLAB:(A + 1) * SLAB, :] = jnp.zeros((half, SLAB, N_POT), F32)
            pass_c(2)

        @pl.when(n == 4)
        def _():
            pass_d(1)

        @pl.when(n == 6)
        def _():
            got_c[2].wait_recv()

        @pl.when(n == 9)
        def _():
            for k in (2, 0, 1):
                got_d[k].wait_recv()

        @pl.when(column == 0)
        def _():
            scale(slot, 0, TIMES)

        tile(column, TIMES)

        @pl.when(column == 2)
        def _():
            apply(slot, 0, TIMES)
        return carry

    lax.fori_loop(0, 12, step, 0)

    pot_far[0:SLAB] = far[OWN, :, N_ORB:] * jnp.asarray(0.5, BF16)
    for slot in (B, C, D, A):
        pot_far[slot * SLAB:(slot + 1) * SLAB] = far[slot, :, N_ORB:]
    used = 5 * SLAB
    pot_far[used:] = jnp.zeros((N_POT - used, N_POT), BF16)
    pot_t = pot_far[...].T
    applied[:, used:, :] = jnp.zeros((TIMES, N_POT - used, N_POT), F32)

    def project(t, carry):
        whole = applied[t]
        high = whole.astype(BF16)
        low = (whole - high.astype(F32)).astype(BF16)
        both = jnp.dot(pot_t, high, preferred_element_type=F32) + jnp.dot(
            pot_t, low, preferred_element_type=F32)
        proj[t, 0:128] = both[:128, :128]
        proj[t, 128:256] = both[:128, 128:] + both[128:, :128].T
        proj[t, 256:384] = both[128:, 128:]
        return carry

    lax.fori_loop(0, TIMES, project, 0)

    def combine(a, w, carry):
        w_zh, w_x = w // 4, w % 4
        weight = [tw_all[tw_at(t), pl.ds(w, 1), :] for t in range(TIMES)]
        for h in range(2):
            for zl in range(2):
                for yy in range(4):
                    rows = pl.ds(((h * 3 + a) * 8 + zl * 4 + yy) * 8, 8)
                    total = weight[0] * proj[0, rows]
                    for t in range(1, TIMES):
                        total = total + weight[t] * proj[t, rows]
                    zz = w_zh * 2 + zl
                    place = ((w_x, yy, zz), (yy, zz, w_x), (zz, w_x, yy))[a]
                    sums[h, a, place[0], place[1], place[2]] = total
        return carry

    swaps = []
    for a in range(3):
        lax.fori_loop(0, TIMES, functools.partial(combine, a), 0)
        swap = pltpu.make_async_remote_copy(
            src_ref=sums.at[1 - core, a], dst_ref=from_core.at[a],
            send_sem=core_sem.at[a], recv_sem=core_sem.at[3 + a],
            device_id=sibling, device_id_type=MESH)
        swap.start()
        swaps.append(swap)
    z = z_hi * 2 + z_lo
    place = (x, y, z)

    def along(axis, index):
        if axis == 0:
            return (pts, z_hi * 4 + index)
        if axis == 1:
            return at(y_=index)
        return at(z_lo_=index % 2, z_hi_=index // 2)

    copies = []
    held = from_core
    wave = [[swap] for swap in swaps]
    for stage, (arrive, left) in enumerate(((arrive1, left1), (arrive2, left2), (arrive3, final), (None, None))):
        fresh = []
        for a in range(3):
            for copy in wave[a]:
                copy.wait_recv()
            if stage == 0:
                from_core[a] = from_core[a] + sums[core, a]
            else:
                source, landed, total = last
                total[a] = source[a, place[(a + stage - 1) % 3]] + landed[a, 0] + landed[a, 1] + landed[a, 2]
            if arrive is None:
                continue
            axis = (a + stage) % 3
            sends = []
            for d in (2, 1, 3):
                index = (place[axis] + d) % 4
                i = (stage * 3 + a) * 3 + d - 1
                copy = pltpu.make_async_remote_copy(
                    src_ref=held.at[a, index], dst_ref=arrive.at[a, d - 1],
                    send_sem=ring_send.at[i], recv_sem=ring_recv.at[i],
                    device_id=along(axis, index), device_id_type=MESH)
                copy.start()
                sends.append(copy)
            fresh.append(sends)
            copies += sends
        wave, last, held = fresh, (held, arrive, left), left

    def spread(i, src, dst, peer):
        copy = pltpu.make_async_remote_copy(
            src_ref=src, dst_ref=dst, send_sem=all_send.at[i], recv_sem=all_recv.at[i],
            device_id=peer, device_id_type=MESH)
        copy.start()
        return copy

    corner = z_lo * 2 + core
    near = [spread(i, final, quad.at[corner], peer) for i, peer in enumerate((z_in_sibling, z_in, sibling))]
    quad[corner] = final[...]
    for copy in near:
        copy.wait_recv()
    wide = [spread(3 + i, quad, whole_out.at[y], peer) for i, peer in enumerate((y_across, y_up, y_down))]
    whole_out[y] = quad[...]
    for copy in wide:
        copy.wait_recv()
    rows = []
    for h in range(2):
        for a in range(3):
            for zl in range(2):
                for yy in range(4):
                    rows.append(whole_out[yy, zl * 2 + h, a])
    low, mid, high = [jnp.concatenate(rows[16 * b:16 * b + 16], axis=0) for b in range(3)]
    out_ref[0, :128, :128] = low + low.T
    out_ref[0, :128, 128:] = mid
    out_ref[0, 128:, :128] = mid.T
    out_ref[0, 128:, 128:] = high + high.T
    for copy in sent + tw_copies + swaps + copies + near + wide:
        copy.wait_send()


def body(occ, virt, pot, occ_energy, virt_energy, times, weights):
    anywhere, vmem = pl.BlockSpec(memory_space=pl.ANY), pl.BlockSpec(memory_space=pltpu.VMEM)
    smem = pl.BlockSpec(memory_space=pltpu.SMEM)
    return pl.pallas_call(
        kernel,
        out_shape=jax.ShapeDtypeStruct((1, N_POT, N_POT), F32),
        in_specs=[anywhere] * 3 + [vmem] * 2 + [smem] * 2,
        out_specs=vmem,
        scratch_shapes=[
            pltpu.VMEM((2 * ROWS, WIDTH), BF16),
            pltpu.VMEM((5, SLAB, WIDTH), BF16),
            pltpu.VMEM((CHUNK, WIDTH), BF16),
            pltpu.VMEM((TIMES * SLAB, N_ORB), BF16),
            pltpu.VMEM((TIMES * SLAB, 2 * ROWS), BF16),
            pltpu.VMEM((TIMES, N_POT, N_POT), F32),
            pltpu.VMEM((TIMES, 1, N_ORB), F32),
            pltpu.VMEM((TIMES, 16, 128), F32),
            pltpu.VMEM((N_POT, N_POT), BF16),
            pltpu.VMEM((TIMES, 384, 128), F32),
            pltpu.VMEM((2, 3, 4, 4, 4, 8, 128), F32),
            pltpu.VMEM((3, 4, 4, 4, 8, 128), F32),
            pltpu.VMEM((3, 3, 4, 4, 8, 128), F32),
            pltpu.VMEM((3, 3, 4, 8, 128), F32),
            pltpu.VMEM((3, 3, 8, 128), F32),
            pltpu.VMEM((3, 4, 4, 8, 128), F32),
            pltpu.VMEM((3, 4, 8, 128), F32),
            pltpu.VMEM((3, 8, 128), F32),
            pltpu.VMEM((4, 3, 8, 128), F32),
            pltpu.VMEM((4, 4, 3, 8, 128), F32),
            pltpu.SemaphoreType.DMA((6,)),
            pltpu.SemaphoreType.DMA((24,)),
            pltpu.SemaphoreType.DMA((24,)),
            pltpu.SemaphoreType.DMA((4,)),
            pltpu.SemaphoreType.DMA((4,)),
            pltpu.SemaphoreType.DMA((6,)),
            pltpu.SemaphoreType.DMA((27,)),
            pltpu.SemaphoreType.DMA((27,)),
            pltpu.SemaphoreType.DMA((6,)),
            pltpu.SemaphoreType.DMA((6,)),
        ],
        compiler_params=pltpu.CompilerParams(
            collective_id=0, has_side_effects=True, vmem_limit_bytes=60 * 2**20),
    )(occ, virt, pot, occ_energy[None, :], virt_energy[None, :], times, weights.T)


def solution(mesh):
    return jax.shard_map(
        body,
        mesh=mesh,
        in_specs=(P("pts", None), P("pts", None), P("pts", None), P(), P(), P("tau"), P(None, "tau")),
        out_specs=P("tau", None, None),
        check_vma=False,
    )
```

time: 75.9 us -> 70.8 us (0.933)
  Pallas kernels: 72 us -> 68.3 us
  local copies, waits for them, and re-layouts: 2.99 us -> 1.67 us
    pallas_call x1, Pallas kernels: 72 us -> 68.3 us  [body(): pl.pallas_call(kernel, out_shape=jax.ShapeDtypeStruct((1, N_POT, N_POT),...]
    unnamed x2 -> x1, local copies, waits for them, and re-layouts: 2.99 us -> 1.67 us
where the time goes in v3:
time: 70.8 us; the launch traced here: 70.6 us
  Pallas kernels  68.3 us (96%)
  local copies, waits for them, and re-layouts  1.67 us (2%)
    pallas_call x1, Pallas kernels, body(): pl.pallas_call(kernel, out_shape=jax.ShapeDtypeStruct((1, N_POT, N_POT),...  68.3 us
    unnamed x1, local copies, waits for them, and re-layouts  1.67 us

profile of v3, /device:TPU:1, one launch (start us, length us, event | category | flops | bytes accessed | tf_op | source)
XLA Modules:
  0.0 70.6 jit_solution(869857046103003521)
XLA Ops:
  0.7 68.3 %shard_map.73 = f32[1,256,256]{2,1,0:T(8,128)} custom-call(bf16[384,2048]{1,0:T(8,128)(2,1)} %occ_ref.1, bf16[384,4096]{1,0:T(8,128)(2,1)} %virt_ref.1, bf16[384,256]{1,0:T(8,128)(2,1)} %pot_ref.1, f32[1,2048]{1,0:T(1,128)} %bitcast.4, f32[1,4096]{1,0:T(1,128)} %bitcast.3, f32[1]{0:T(128)S(6)} %copy.9.times_ref, f32[1,8]{1,0:T(1,128)} %bitcast.5), custom_call_target="tpu_custom_call" | custom-call | tf_op jit(solution)/shard_map/pallas_call | solution.py:347
  68.9 1.7 %copy.10 = f32[1,256,256]{2,1,0:T(8,128)} copy(f32[1,256,256]{2,1,0:T(8,128)} %shard_map.73) | data formatting | bytes 524288

commit v4 on v3

--- a/solution.py
+++ b/solution.py
@@ -23,9 +23,9 @@
 def kernel(
     occ_ref, virt_ref, pot_ref, occ_e_ref, virt_e_ref, times_ref, weights_ref, out_ref,
     own, far, relay, scaled, resp, applied, factor, tw_all, pot_far, proj,
-    sums, from_core, arrive1, arrive2, arrive3, left1, left2, final, quad, whole_out,
+    sums, from_core, arrive1, arrive2, left1, final, whole_out,
     load_sem, send_sem, recv_sem, tw_send, tw_recv,
-    core_sem, ring_send, ring_recv, all_send, all_recv,
+    core_sem, ring_send, ring_recv, plane_sem, all_send, all_recv,
 ):
     pts, tau = lax.axis_index("pts"), lax.axis_index("tau")
     z_lo, y, core = pts // 8, (pts // 2) % 4, pts % 2
@@ -43,10 +43,17 @@
     z_in = at(z_lo_=1 - z_lo)
     y_down = at(y_=(y + 3) % 4)
     y_up = at(y_=(y + 1) % 4)
-    z_in_sibling = at(z_lo_=1 - z_lo, core_=1 - core)
-    z_far = at(z_hi_=1 - z_hi)
-    x_peers = [(pts, z_hi * 4 + (x + d) % 4) for d in range(1, 4)]
-    y_across = at(y_=(y + 2) % 4)
+    tau_peers = [(pts, (tau + d) % TIMES) for d in range(1, TIMES)]
+    place = (x, y, z_hi * 2 + z_lo)
+
+    def device(x_, y_, z_):
+        return ((z_ % 2) * 8 + y_ * 2 + core, (z_ // 2) * 4 + x_)
+
+    def off(*steps):
+        return device(*[(p + d) % 4 for p, d in zip(place, steps)])
+
+    in_planes = [
+        off(i // 16, i // 4 % 4, i % 4) for i in range(1, 64) if 0 in (i // 16, i // 4 % 4, i % 4)]
 
     first = pl.multiple_of(tau * SLAB, CHUNK)
     parts = ((occ_ref, 0, N_OCC), (virt_ref, N_OCC, N_VIRT), (pot_ref, N_ORB, N_POT))
@@ -61,13 +68,12 @@
         load.start()
 
     barrier = pltpu.get_barrier_semaphore()
-    greeted = [sibling, z_in, z_in_sibling, z_out, z_far, y_down, y_up, y_across] + x_peers
+    greeted = [sibling] + in_planes
     for peer in greeted:
         pl.semaphore_signal(barrier, 1, device_id=peer, device_id_type=MESH)
-    here = x * 2 + z_hi
     for w in range(TIMES):
-        tw_all[here, w:w + 1] = jnp.full((1, 128), weights_ref[0, w], F32)
-    tw_all[here, 8:16] = jnp.full((8, 128), times_ref[0], F32)
+        tw_all[tau, w:w + 1] = jnp.full((1, 128), weights_ref[0, w], F32)
+    tw_all[tau, 8:16] = jnp.full((8, 128), times_ref[0], F32)
     pl.semaphore_wait(barrier, len(greeted))
 
     count = iter(range(64))
@@ -86,14 +92,13 @@
         copy.start()
         return copy
 
-    def send_tw(i, first, tiles, peer):
+    tw_copies = []
+    for i, peer in enumerate(tau_peers):
         copy = pltpu.make_async_remote_copy(
-            src_ref=tw_all.at[pl.ds(first, tiles)], dst_ref=tw_all.at[pl.ds(first, tiles)],
-            send_sem=tw_send.at[i], recv_sem=tw_recv.at[i], device_id=peer, device_id_type=MESH)
+            src_ref=tw_all.at[tau], dst_ref=tw_all.at[tau], send_sem=tw_send.at[i], recv_sem=tw_recv.at[i],
+            device_id=peer, device_id_type=MESH)
         copy.start()
-        return copy
-
-    tw_copies = [send_tw(0, here, 1, z_far)]
+        tw_copies.append(copy)
 
     def rows_of(k):
         return pl.ds(k * CHUNK, CHUNK)
@@ -115,16 +120,10 @@
     }
     got_own = send(own.at[pl.ds(0, ROWS)], own.at[pl.ds(ROWS, ROWS)], sibling)
 
-    tw_copies[0].wait_recv()
-    tw_copies += [send_tw(1 + i, x * 2, 2, peer) for i, peer in enumerate(x_peers)]
-    for copy in tw_copies[1:]:
+    for copy in tw_copies:
         copy.wait_recv()
-
-    def tw_at(t):
-        return (t % 4) * 2 + t // 4
-
     for t in range(TIMES):
-        moment = tw_all[tw_at(t), 8:9, 0:1]
+        moment = tw_all[t, 8:9, 0:1]
         factor[t, :, :N_OCC] = jnp.exp(moment * occ_e_ref[...])
         factor[t, :, N_OCC:] = jnp.exp(-moment * virt_e_ref[...])
 
@@ -181,14 +180,20 @@
         tile(n, half)
         return carry
 
-    def step(n, carry):
-        slot, column = n // 3, n % 3
-
-        @pl.when(n == 1)
+    def full_tile(slot, column, carry):
+        @pl.when((slot == OWN) & (column == 1))
         def _():
             got_own.wait_recv()
 
-        @pl.when(n == 3)
+        @pl.when((slot == B) & (column == 1))
+        def _():
+            pass_d(1)
+
+        tile(column, TIMES)
+        return carry
+
+    def step(slot, carry):
+        @pl.when(slot == B)
         def _():
             pass_c(1)
             got_a[1].wait_recv()
@@ -199,31 +204,21 @@
             applied[pl.ds(t_other, half), A * SLAB:(A + 1) * SLAB, :] = jnp.zeros((half, SLAB, N_POT), F32)
             pass_c(2)
 
-        @pl.when(n == 4)
-        def _():
-            pass_d(1)
-
-        @pl.when(n == 6)
+        @pl.when(slot == C)
         def _():
             got_c[2].wait_recv()
 
-        @pl.when(n == 9)
+        @pl.when(slot == D)
         def _():
             for k in (2, 0, 1):
                 got_d[k].wait_recv()
 
-        @pl.when(column == 0)
-        def _():
-            scale(slot, 0, TIMES)
-
-        tile(column, TIMES)
-
-        @pl.when(column == 2)
-        def _():
-            apply(slot, 0, TIMES)
-        return carry
-
-    lax.fori_loop(0, 12, step, 0)
+        scale(slot, 0, TIMES)
+        lax.fori_loop(0, 3, functools.partial(full_tile, slot), 0)
+        apply(slot, 0, TIMES)
+        return carry
+
+    lax.fori_loop(0, 4, step, 0)
 
     pot_far[0:SLAB] = far[OWN, :, N_ORB:] * jnp.asarray(0.5, BF16)
     for slot in (B, C, D, A):
@@ -246,69 +241,74 @@
 
     lax.fori_loop(0, TIMES, project, 0)
 
-    def combine(a, w, carry):
+    def combine(h, a, w, carry):
         w_zh, w_x = w // 4, w % 4
-        weight = [tw_all[tw_at(t), pl.ds(w, 1), :] for t in range(TIMES)]
-        for h in range(2):
-            for zl in range(2):
-                for yy in range(4):
-                    rows = pl.ds(((h * 3 + a) * 8 + zl * 4 + yy) * 8, 8)
-                    total = weight[0] * proj[0, rows]
-                    for t in range(1, TIMES):
-                        total = total + weight[t] * proj[t, rows]
-                    zz = w_zh * 2 + zl
-                    place = ((w_x, yy, zz), (yy, zz, w_x), (zz, w_x, yy))[a]
-                    sums[h, a, place[0], place[1], place[2]] = total
+        weight = [tw_all[t, pl.ds(w, 1), :] for t in range(TIMES)]
+        for zl in range(2):
+            for yy in range(4):
+                rows = pl.ds(pl.multiple_of(((h * 3 + a) * 8 + zl * 4 + yy) * 8, 8), 8)
+                total = weight[0] * proj[0, rows]
+                for t in range(1, TIMES):
+                    total = total + weight[t] * proj[t, rows]
+                zz = w_zh * 2 + zl
+                spot = ((w_x, yy, zz), (yy, zz, w_x), (zz, w_x, yy))[a]
+                sums[h, a, spot[0], spot[1], spot[2]] = total
         return carry
 
     swaps = []
     for a in range(3):
-        lax.fori_loop(0, TIMES, functools.partial(combine, a), 0)
+        lax.fori_loop(0, TIMES, functools.partial(combine, 1 - core, a), 0)
         swap = pltpu.make_async_remote_copy(
             src_ref=sums.at[1 - core, a], dst_ref=from_core.at[a],
             send_sem=core_sem.at[a], recv_sem=core_sem.at[3 + a],
             device_id=sibling, device_id_type=MESH)
         swap.start()
         swaps.append(swap)
-    z = z_hi * 2 + z_lo
-    place = (x, y, z)
-
-    def along(axis, index):
-        if axis == 0:
-            return (pts, z_hi * 4 + index)
-        if axis == 1:
-            return at(y_=index)
-        return at(z_lo_=index % 2, z_hi_=index // 2)
-
     copies = []
-    held = from_core
-    wave = [[swap] for swap in swaps]
-    for stage, (arrive, left) in enumerate(((arrive1, left1), (arrive2, left2), (arrive3, final), (None, None))):
-        fresh = []
-        for a in range(3):
-            for copy in wave[a]:
-                copy.wait_recv()
-            if stage == 0:
-                from_core[a] = from_core[a] + sums[core, a]
-            else:
-                source, landed, total = last
-                total[a] = source[a, place[(a + stage - 1) % 3]] + landed[a, 0] + landed[a, 1] + landed[a, 2]
-            if arrive is None:
-                continue
-            axis = (a + stage) % 3
-            sends = []
-            for d in (2, 1, 3):
-                index = (place[axis] + d) % 4
-                i = (stage * 3 + a) * 3 + d - 1
-                copy = pltpu.make_async_remote_copy(
-                    src_ref=held.at[a, index], dst_ref=arrive.at[a, d - 1],
-                    send_sem=ring_send.at[i], recv_sem=ring_recv.at[i],
-                    device_id=along(axis, index), device_id_type=MESH)
-                copy.start()
-                sends.append(copy)
-            fresh.append(sends)
-            copies += sends
-        wave, last, held = fresh, (held, arrive, left), left
+    wave = []
+    for a in range(3):
+        lax.fori_loop(0, TIMES, functools.partial(combine, core, a), 0)
+        swaps[a].wait_recv()
+        from_core[a] = from_core[a] + sums[core, a]
+        sends = []
+        for d in (2, 1, 3):
+            index = (place[a] + d) % 4
+            i = a * 3 + d - 1
+            copy = pltpu.make_async_remote_copy(
+                src_ref=from_core.at[a, index], dst_ref=arrive1.at[a, d - 1],
+                send_sem=ring_send.at[i], recv_sem=ring_recv.at[i],
+                device_id=device(*[index if k == a else place[k] for k in range(3)]), device_id_type=MESH)
+            copy.start()
+            sends.append(copy)
+        wave.append(sends)
+        copies += sends
+    planes = []
+    for a in range(3):
+        for copy in wave[a]:
+            copy.wait_recv()
+        left1[a] = from_core[a, place[a]] + arrive1[a, 0] + arrive1[a, 1] + arrive1[a, 2]
+
+        def fan(d, carry):
+            spot = list(place)
+            second, third = (a + 1) % 3, (a + 2) % 3
+            spot[second] = (place[second] + d // 4) % 4
+            spot[third] = (place[third] + d % 4) % 4
+            pltpu.make_async_remote_copy(
+                src_ref=left1.at[a, spot[second], spot[third]], dst_ref=arrive2.at[a, d - 1],
+                send_sem=plane_sem.at[a], recv_sem=plane_sem.at[3 + a],
+                device_id=device(*spot), device_id_type=MESH).start()
+            return carry
+
+        lax.fori_loop(1, 16, fan, 0)
+        planes.append(pltpu.make_async_remote_copy(
+            src_ref=arrive2.at[a], dst_ref=arrive2.at[a], send_sem=plane_sem.at[a],
+            recv_sem=plane_sem.at[3 + a], device_id=sibling, device_id_type=MESH))
+    for a in range(3):
+        planes[a].wait_recv()
+        total = left1[a, place[(a + 1) % 3], place[(a + 2) % 3]]
+        for d in range(15):
+            total = total + arrive2[a, d]
+        final[a] = total
 
     def spread(i, src, dst, peer):
         copy = pltpu.make_async_remote_copy(
@@ -317,27 +317,27 @@
         copy.start()
         return copy
 
-    corner = z_lo * 2 + core
-    near = [spread(i, final, quad.at[corner], peer) for i, peer in enumerate((z_in_sibling, z_in, sibling))]
-    quad[corner] = final[...]
-    for copy in near:
-        copy.wait_recv()
-    wide = [spread(3 + i, quad, whole_out.at[y], peer) for i, peer in enumerate((y_across, y_up, y_down))]
-    whole_out[y] = quad[...]
+    corner = z_lo * 4 + y
+    wide = [
+        spread(i, final, whole_out.at[core, corner], at(z_lo_=(z_lo + (i + 1) // 4) % 2, y_=(y + (i + 1) % 4) % 4))
+        for i in range(7)]
+    whole_out[core, corner] = final[...]
     for copy in wide:
         copy.wait_recv()
+    near = [spread(7, whole_out.at[core], whole_out.at[core], sibling)]
+    near[0].wait_recv()
     rows = []
     for h in range(2):
         for a in range(3):
             for zl in range(2):
                 for yy in range(4):
-                    rows.append(whole_out[yy, zl * 2 + h, a])
+                    rows.append(whole_out[h, zl * 4 + yy, a])
     low, mid, high = [jnp.concatenate(rows[16 * b:16 * b + 16], axis=0) for b in range(3)]
     out_ref[0, :128, :128] = low + low.T
     out_ref[0, :128, 128:] = mid
     out_ref[0, 128:, :128] = mid.T
     out_ref[0, 128:, 128:] = high + high.T
-    for copy in sent + tw_copies + swaps + copies + near + wide:
+    for copy in sent + tw_copies + swaps + copies + planes + near + wide:
         copy.wait_send()
 
 
@@ -363,23 +363,21 @@
             pltpu.VMEM((2, 3, 4, 4, 4, 8, 128), F32),
             pltpu.VMEM((3, 4, 4, 4, 8, 128), F32),
             pltpu.VMEM((3, 3, 4, 4, 8, 128), F32),
-            pltpu.VMEM((3, 3, 4, 8, 128), F32),
-            pltpu.VMEM((3, 3, 8, 128), F32),
+            pltpu.VMEM((3, 15, 8, 128), F32),
             pltpu.VMEM((3, 4, 4, 8, 128), F32),
-            pltpu.VMEM((3, 4, 8, 128), F32),
             pltpu.VMEM((3, 8, 128), F32),
-            pltpu.VMEM((4, 3, 8, 128), F32),
-            pltpu.VMEM((4, 4, 3, 8, 128), F32),
+            pltpu.VMEM((2, 8, 3, 8, 128), F32),
             pltpu.SemaphoreType.DMA((6,)),
             pltpu.SemaphoreType.DMA((24,)),
             pltpu.SemaphoreType.DMA((24,)),
-            pltpu.SemaphoreType.DMA((4,)),
-            pltpu.SemaphoreType.DMA((4,)),
+            pltpu.SemaphoreType.DMA((7,)),
+            pltpu.SemaphoreType.DMA((7,)),
             pltpu.SemaphoreType.DMA((6,)),
-            pltpu.SemaphoreType.DMA((27,)),
-            pltpu.SemaphoreType.DMA((27,)),
+            pltpu.SemaphoreType.DMA((9,)),
+            pltpu.SemaphoreType.DMA((9,)),
             pltpu.SemaphoreType.DMA((6,)),
-            pltpu.SemaphoreType.DMA((6,)),
+            pltpu.SemaphoreType.DMA((8,)),
+            pltpu.SemaphoreType.DMA((8,)),
         ],
         compiler_params=pltpu.CompilerParams(
             collective_id=0, has_side_effects=True, vmem_limit_bytes=60 * 2**20),

time: 70.8 us -> 69.5 us (0.982)
  Pallas kernels: 68.3 us -> 67 us
    pallas_call x1, Pallas kernels: 68.3 us -> 67 us  [body(): pl.pallas_call(kernel, out_shape=jax.ShapeDtypeStruct((1, N_POT, N_POT),...]
where the time goes in v4:
time: 69.5 us; the launch traced here: 69.3 us
  Pallas kernels  67 us (96%)
  local copies, waits for them, and re-layouts  1.67 us (2%)
    pallas_call x1, Pallas kernels, body(): pl.pallas_call(kernel, out_shape=jax.ShapeDtypeStruct((1, N_POT, N_POT),...  67 us
    unnamed x1, local copies, waits for them, and re-layouts  1.67 us

profile of v4, /device:TPU:1, one launch (start us, length us, event | category | flops | bytes accessed | tf_op | source)
XLA Modules:
  0.0 69.3 jit_solution(2808635407130114173)
XLA Ops:
  0.7 67.0 %shard_map.73 = f32[1,256,256]{2,1,0:T(8,128)} custom-call(bf16[384,2048]{1,0:T(8,128)(2,1)} %occ_ref.1, bf16[384,4096]{1,0:T(8,128)(2,1)} %virt_ref.1, bf16[384,256]{1,0:T(8,128)(2,1)} %pot_ref.1, f32[1,2048]{1,0:T(1,128)} %bitcast.4, f32[1,4096]{1,0:T(1,128)} %bitcast.3, f32[1]{0:T(128)S(6)} %copy.9.times_ref, f32[1,8]{1,0:T(1,128)} %bitcast.5), custom_call_target="tpu_custom_call" | custom-call | tf_op jit(solution)/shard_map/pallas_call | solution.py:347
  67.6 1.7 %copy.10 = f32[1,256,256]{2,1,0:T(8,128)} copy(f32[1,256,256]{2,1,0:T(8,128)} %shard_map.73) | data formatting | bytes 524288

commit v5 on v4

--- a/solution.py
+++ b/solution.py
@@ -43,14 +43,17 @@
     z_in = at(z_lo_=1 - z_lo)
     y_down = at(y_=(y + 3) % 4)
     y_up = at(y_=(y + 1) % 4)
-    tau_peers = [(pts, (tau + d) % TIMES) for d in range(1, TIMES)]
+    tau_peers = [
+        (pts, ((z_hi + dz) % 2) * 4 + (x + dx) % 4)
+        for dz, dx in ((1, 2), (1, 1), (1, 3), (1, 0), (0, 2), (0, 1), (0, 3))]
     place = (x, y, z_hi * 2 + z_lo)
 
-    def device(x_, y_, z_):
-        return ((z_ % 2) * 8 + y_ * 2 + core, (z_ // 2) * 4 + x_)
+    ahead = [[lax.rem(p + d, 4) for d in range(4)] for p in place]
+    in_pts = [[0] * 4, [2 * c + core for c in ahead[1]], [8 * lax.rem(c, 2) for c in ahead[2]]]
+    in_tau = [ahead[0], [0] * 4, [4 * lax.div(c, 2) for c in ahead[2]]]
 
     def off(*steps):
-        return device(*[(p + d) % 4 for p, d in zip(place, steps)])
+        return (in_pts[1][steps[1]] + in_pts[2][steps[2]], in_tau[0][steps[0]] + in_tau[2][steps[2]])
 
     in_planes = [
         off(i // 16, i // 4 % 4, i % 4) for i in range(1, 64) if 0 in (i // 16, i // 4 % 4, i % 4)]
@@ -239,7 +242,7 @@
         proj[t, 256:384] = both[128:, 128:]
         return carry
 
-    lax.fori_loop(0, TIMES, project, 0)
+    lax.fori_loop(0, TIMES, project, 0, unroll=4)
 
     def combine(h, a, w, carry):
         w_zh, w_x = w // 4, w % 4
@@ -272,34 +275,31 @@
         from_core[a] = from_core[a] + sums[core, a]
         sends = []
         for d in (2, 1, 3):
-            index = (place[a] + d) % 4
             i = a * 3 + d - 1
             copy = pltpu.make_async_remote_copy(
-                src_ref=from_core.at[a, index], dst_ref=arrive1.at[a, d - 1],
+                src_ref=from_core.at[a, ahead[a][d]], dst_ref=arrive1.at[a, d - 1],
                 send_sem=ring_send.at[i], recv_sem=ring_recv.at[i],
-                device_id=device(*[index if k == a else place[k] for k in range(3)]), device_id_type=MESH)
+                device_id=off(*[d if k == a else 0 for k in range(3)]), device_id_type=MESH)
             copy.start()
             sends.append(copy)
         wave.append(sends)
         copies += sends
+    for copy in sent + tw_copies:
+        copy.wait_send()
     planes = []
     for a in range(3):
         for copy in wave[a]:
             copy.wait_recv()
         left1[a] = from_core[a, place[a]] + arrive1[a, 0] + arrive1[a, 1] + arrive1[a, 2]
 
-        def fan(d, carry):
-            spot = list(place)
-            second, third = (a + 1) % 3, (a + 2) % 3
-            spot[second] = (place[second] + d // 4) % 4
-            spot[third] = (place[third] + d % 4) % 4
+        second, third = (a + 1) % 3, (a + 2) % 3
+        for d in range(1, 16):
+            steps = [0] * 3
+            steps[second], steps[third] = d // 4, d % 4
             pltpu.make_async_remote_copy(
-                src_ref=left1.at[a, spot[second], spot[third]], dst_ref=arrive2.at[a, d - 1],
+                src_ref=left1.at[a, ahead[second][d // 4], ahead[third][d % 4]], dst_ref=arrive2.at[a, d - 1],
                 send_sem=plane_sem.at[a], recv_sem=plane_sem.at[3 + a],
-                device_id=device(*spot), device_id_type=MESH).start()
-            return carry
-
-        lax.fori_loop(1, 16, fan, 0)
+                device_id=off(*steps), device_id_type=MESH).start()
         planes.append(pltpu.make_async_remote_copy(
             src_ref=arrive2.at[a], dst_ref=arrive2.at[a], send_sem=plane_sem.at[a],
             recv_sem=plane_sem.at[3 + a], device_id=sibling, device_id_type=MESH))
@@ -325,6 +325,8 @@
     for copy in wide:
         copy.wait_recv()
     near = [spread(7, whole_out.at[core], whole_out.at[core], sibling)]
+    for copy in swaps + copies + planes + wide:
+        copy.wait_send()
     near[0].wait_recv()
     rows = []
     for h in range(2):
@@ -337,7 +339,7 @@
     out_ref[0, :128, 128:] = mid
     out_ref[0, 128:, :128] = mid.T
     out_ref[0, 128:, 128:] = high + high.T
-    for copy in sent + tw_copies + swaps + copies + planes + near + wide:
+    for copy in near:
         copy.wait_send()
 
 

time: 69.5 us -> 67.7 us (0.974)
  Pallas kernels: 67 us -> 65.2 us
    pallas_call x1, Pallas kernels: 67 us -> 65.2 us  [body(): pl.pallas_call(kernel, out_shape=jax.ShapeDtypeStruct((1, N_POT, N_POT),...]
where the time goes in v5:
time: 67.7 us; the launch traced here: 67.5 us
  Pallas kernels  65.2 us (96%)
  local copies, waits for them, and re-layouts  1.67 us (2%)
    pallas_call x1, Pallas kernels, body(): pl.pallas_call(kernel, out_shape=jax.ShapeDtypeStruct((1, N_POT, N_POT),...  65.2 us
    unnamed x1, local copies, waits for them, and re-layouts  1.67 us

profile of v5, /device:TPU:1, one launch (start us, length us, event | category | flops | bytes accessed | tf_op | source)
XLA Modules:
  0.0 67.5 jit_solution(18322177301795077711)
XLA Ops:
  0.7 65.2 %shard_map.73 = f32[1,256,256]{2,1,0:T(8,128)} custom-call(bf16[384,2048]{1,0:T(8,128)(2,1)} %occ_ref.1, bf16[384,4096]{1,0:T(8,128)(2,1)} %virt_ref.1, bf16[384,256]{1,0:T(8,128)(2,1)} %pot_ref.1, f32[1,2048]{1,0:T(1,128)} %bitcast.4, f32[1,4096]{1,0:T(1,128)} %bitcast.3, f32[1]{0:T(128)S(6)} %copy.9.times_ref, f32[1,8]{1,0:T(1,128)} %bitcast.5), custom_call_target="tpu_custom_call" | custom-call | tf_op jit(solution)/shard_map/pallas_call | solution.py:349
  65.9 1.7 %copy.10 = f32[1,256,256]{2,1,0:T(8,128)} copy(f32[1,256,256]{2,1,0:T(8,128)} %shard_map.73) | data formatting | bytes 524288

commit v6 on v5

--- a/solution.py
+++ b/solution.py
@@ -71,7 +71,8 @@
         load.start()
 
     barrier = pltpu.get_barrier_semaphore()
-    greeted = [sibling] + in_planes
+    across = [at(z_lo_=lax.rem(z_lo + d // 4, 2), y_=ahead[1][d % 4], core_=1 - core) for d in range(1, 8)]
+    greeted = [sibling] + in_planes + across
     for peer in greeted:
         pl.semaphore_signal(barrier, 1, device_id=peer, device_id_type=MESH)
     for w in range(TIMES):
@@ -242,7 +243,7 @@
         proj[t, 256:384] = both[128:, 128:]
         return carry
 
-    lax.fori_loop(0, TIMES, project, 0, unroll=4)
+    lax.fori_loop(0, TIMES, project, 0, unroll=8)
 
     def combine(h, a, w, carry):
         w_zh, w_x = w // 4, w % 4
@@ -260,7 +261,7 @@
 
     swaps = []
     for a in range(3):
-        lax.fori_loop(0, TIMES, functools.partial(combine, 1 - core, a), 0)
+        lax.fori_loop(0, TIMES, functools.partial(combine, 1 - core, a), 0, unroll=2)
         swap = pltpu.make_async_remote_copy(
             src_ref=sums.at[1 - core, a], dst_ref=from_core.at[a],
             send_sem=core_sem.at[a], recv_sem=core_sem.at[3 + a],
@@ -270,7 +271,7 @@
     copies = []
     wave = []
     for a in range(3):
-        lax.fori_loop(0, TIMES, functools.partial(combine, core, a), 0)
+        lax.fori_loop(0, TIMES, functools.partial(combine, core, a), 0, unroll=2)
         swaps[a].wait_recv()
         from_core[a] = from_core[a] + sums[core, a]
         sends = []
@@ -318,16 +319,17 @@
         return copy
 
     corner = z_lo * 4 + y
-    wide = [
-        spread(i, final, whole_out.at[core, corner], at(z_lo_=(z_lo + (i + 1) // 4) % 2, y_=(y + (i + 1) % 4) % 4))
-        for i in range(7)]
+    wide = []
+    for i in range(15):
+        d, other = (i + 1) % 8, (i + 1) // 8
+        peer = at(z_lo_=lax.rem(z_lo + d // 4, 2), y_=ahead[1][d % 4], core_=1 - core if other else core)
+        wide.append(spread(i, final, whole_out.at[core, corner], peer))
+    near = []
     whole_out[core, corner] = final[...]
+    for copy in swaps + copies + planes:
+        copy.wait_send()
     for copy in wide:
         copy.wait_recv()
-    near = [spread(7, whole_out.at[core], whole_out.at[core], sibling)]
-    for copy in swaps + copies + planes + wide:
-        copy.wait_send()
-    near[0].wait_recv()
     rows = []
     for h in range(2):
         for a in range(3):
@@ -339,7 +341,7 @@
     out_ref[0, :128, 128:] = mid
     out_ref[0, 128:, :128] = mid.T
     out_ref[0, 128:, 128:] = high + high.T
-    for copy in near:
+    for copy in wide:
         copy.wait_send()
 
 
@@ -378,8 +380,8 @@
             pltpu.SemaphoreType.DMA((9,)),
             pltpu.SemaphoreType.DMA((9,)),
             pltpu.SemaphoreType.DMA((6,)),
-            pltpu.SemaphoreType.DMA((8,)),
-            pltpu.SemaphoreType.DMA((8,)),
+            pltpu.SemaphoreType.DMA((15,)),
+            pltpu.SemaphoreType.DMA((15,)),
         ],
         compiler_params=pltpu.CompilerParams(
             collective_id=0, has_side_effects=True, vmem_limit_bytes=60 * 2**20),

time: 67.7 us -> 66.3 us (0.979)
  Pallas kernels: 65.2 us -> 63.8 us
    pallas_call x1, Pallas kernels: 65.2 us -> 63.8 us  [body(): pl.pallas_call(kernel, out_shape=jax.ShapeDtypeStruct((1, N_POT, N_POT),...]
where the time goes in v6:
time: 66.3 us; the launch traced here: 66.2 us
  Pallas kernels  63.8 us (96%)
  local copies, waits for them, and re-layouts  1.67 us (3%)
    pallas_call x1, Pallas kernels, body(): pl.pallas_call(kernel, out_shape=jax.ShapeDtypeStruct((1, N_POT, N_POT),...  63.8 us
    unnamed x1, local copies, waits for them, and re-layouts  1.67 us

profile of v6, /device:TPU:1, one launch (start us, length us, event | category | flops | bytes accessed | tf_op | source)
XLA Modules:
  0.0 66.2 jit_solution(3921810677715685125)
XLA Ops:
  0.7 63.8 %shard_map.73 = f32[1,256,256]{2,1,0:T(8,128)} custom-call(bf16[384,2048]{1,0:T(8,128)(2,1)} %occ_ref.1, bf16[384,4096]{1,0:T(8,128)(2,1)} %virt_ref.1, bf16[384,256]{1,0:T(8,128)(2,1)} %pot_ref.1, f32[1,2048]{1,0:T(1,128)} %bitcast.4, f32[1,4096]{1,0:T(1,128)} %bitcast.3, f32[1]{0:T(128)S(6)} %copy.9.times_ref, f32[1,8]{1,0:T(1,128)} %bitcast.5), custom_call_target="tpu_custom_call" | custom-call | tf_op jit(solution)/shard_map/pallas_call | solution.py:351
  64.5 1.7 %copy.10 = f32[1,256,256]{2,1,0:T(8,128)} copy(f32[1,256,256]{2,1,0:T(8,128)} %shard_map.73) | data formatting | bytes 524288

commit v7 on v6

--- a/solution.py
+++ b/solution.py
@@ -131,6 +131,15 @@
         factor[t, :, :N_OCC] = jnp.exp(moment * occ_e_ref[...])
         factor[t, :, N_OCC:] = jnp.exp(-moment * virt_e_ref[...])
 
+    def scale_chunks(slot, k_first, k_end):
+        def one(i, carry):
+            k, t = i // TIMES, i % TIMES
+            rows = pl.ds(pl.multiple_of(k * CHUNK, CHUNK), CHUNK)
+            wide = far[slot, rows, pl.ds(0, N_ORB)].astype(F32) * factor[t]
+            scaled[pl.ds(pl.multiple_of(t * SLAB + k * CHUNK, CHUNK), CHUNK)] = wide.astype(BF16)
+            return carry
+        lax.fori_loop(k_first * TIMES, k_end * TIMES, one, 0)
+
     def scale(slot, t_first, t_count):
         def one(i, carry):
             rows = pl.ds(pl.multiple_of((i % CHUNKS) * CHUNK, CHUNK), CHUNK)
@@ -206,18 +215,24 @@
             lax.fori_loop(0, 3, half_tile, 0)
             apply(A, t_mine, half)
             applied[pl.ds(t_other, half), A * SLAB:(A + 1) * SLAB, :] = jnp.zeros((half, SLAB, N_POT), F32)
-            pass_c(2)
-
-        @pl.when(slot == C)
-        def _():
-            got_c[2].wait_recv()
 
         @pl.when(slot == D)
         def _():
             for k in (2, 0, 1):
                 got_d[k].wait_recv()
 
-        scale(slot, 0, TIMES)
+
+        scale_chunks(slot, 0, 2)
+
+        @pl.when(slot == B)
+        def _():
+            pass_c(2)
+
+        @pl.when(slot == C)
+        def _():
+            got_c[2].wait_recv()
+
+        scale_chunks(slot, 2, CHUNKS)
         lax.fori_loop(0, 3, functools.partial(full_tile, slot), 0)
         apply(slot, 0, TIMES)
         return carry

time: 66.3 us -> 66 us (level)
  no operation moved by 1% of the time
where the time goes in v7:
time: 66 us; the launch traced here: 65.8 us
  Pallas kernels  63.5 us (96%)
  local copies, waits for them, and re-layouts  1.67 us (3%)
  between operations  0.66 us (1%)
    pallas_call x1, Pallas kernels, body(): pl.pallas_call(kernel, out_shape=jax.ShapeDtypeStruct((1, N_POT, N_POT),...  63.5 us
    unnamed x1, local copies, waits for them, and re-layouts  1.67 us

profile of v7, /device:TPU:1, one launch (start us, length us, event | category | flops | bytes accessed | tf_op | source)
XLA Modules:
  0.0 65.8 jit_solution(16433094071876385781)
XLA Ops:
  0.7 63.5 %shard_map.73 = f32[1,256,256]{2,1,0:T(8,128)} custom-call(bf16[384,2048]{1,0:T(8,128)(2,1)} %occ_ref.1, bf16[384,4096]{1,0:T(8,128)(2,1)} %virt_ref.1, bf16[384,256]{1,0:T(8,128)(2,1)} %pot_ref.1, f32[1,2048]{1,0:T(1,128)} %bitcast.4, f32[1,4096]{1,0:T(1,128)} %bitcast.3, f32[1]{0:T(128)S(6)} %copy.9.times_ref, f32[1,8]{1,0:T(1,128)} %bitcast.5), custom_call_target="tpu_custom_call" | custom-call | tf_op jit(solution)/shard_map/pallas_call | solution.py:366
  64.2 1.7 %copy.10 = f32[1,256,256]{2,1,0:T(8,128)} copy(f32[1,256,256]{2,1,0:T(8,128)} %shard_map.73) | data formatting | bytes 524288

commit v8 on v7

--- a/solution.py
+++ b/solution.py
@@ -124,6 +124,10 @@
     }
     got_own = send(own.at[pl.ds(0, ROWS)], own.at[pl.ds(ROWS, ROWS)], sibling)
 
+    pot_far[0:SLAB] = far[OWN, :, N_ORB:] * jnp.asarray(0.5, BF16)
+    used = 5 * SLAB
+    pot_far[used:] = jnp.zeros((N_POT - used, N_POT), BF16)
+    applied[:, used:, :] = jnp.zeros((TIMES, N_POT - used, N_POT), F32)
     for copy in tw_copies:
         copy.wait_recv()
     for t in range(TIMES):
@@ -132,13 +136,17 @@
         factor[t, :, N_OCC:] = jnp.exp(-moment * virt_e_ref[...])
 
     def scale_chunks(slot, k_first, k_end):
+        pieces, span = 6, N_ORB // 6
+
         def one(i, carry):
-            k, t = i // TIMES, i % TIMES
-            rows = pl.ds(pl.multiple_of(k * CHUNK, CHUNK), CHUNK)
-            wide = far[slot, rows, pl.ds(0, N_ORB)].astype(F32) * factor[t]
-            scaled[pl.ds(pl.multiple_of(t * SLAB + k * CHUNK, CHUNK), CHUNK)] = wide.astype(BF16)
+            k = i // pieces
+            lanes = pl.ds(pl.multiple_of((i % pieces) * span, 128), span)
+            wide = far[slot, pl.ds(pl.multiple_of(k * CHUNK, CHUNK), CHUNK), lanes].astype(F32)
+            for t in range(TIMES):
+                rows = pl.ds(pl.multiple_of(t * SLAB + k * CHUNK, CHUNK), CHUNK)
+                scaled[rows, lanes] = (wide * factor[t, :, lanes]).astype(BF16)
             return carry
-        lax.fori_loop(k_first * TIMES, k_end * TIMES, one, 0)
+        lax.fori_loop(k_first * pieces, k_end * pieces, one, 0)
 
     def scale(slot, t_first, t_count):
         def one(i, carry):
@@ -239,13 +247,9 @@
 
     lax.fori_loop(0, 4, step, 0)
 
-    pot_far[0:SLAB] = far[OWN, :, N_ORB:] * jnp.asarray(0.5, BF16)
     for slot in (B, C, D, A):
         pot_far[slot * SLAB:(slot + 1) * SLAB] = far[slot, :, N_ORB:]
-    used = 5 * SLAB
-    pot_far[used:] = jnp.zeros((N_POT - used, N_POT), BF16)
     pot_t = pot_far[...].T
-    applied[:, used:, :] = jnp.zeros((TIMES, N_POT - used, N_POT), F32)
 
     def project(t, carry):
         whole = applied[t]
@@ -276,7 +280,7 @@
 
     swaps = []
     for a in range(3):
-        lax.fori_loop(0, TIMES, functools.partial(combine, 1 - core, a), 0, unroll=2)
+        lax.fori_loop(0, TIMES, functools.partial(combine, 1 - core, a), 0, unroll=4)
         swap = pltpu.make_async_remote_copy(
             src_ref=sums.at[1 - core, a], dst_ref=from_core.at[a],
             send_sem=core_sem.at[a], recv_sem=core_sem.at[3 + a],
@@ -286,7 +290,7 @@
     copies = []
     wave = []
     for a in range(3):
-        lax.fori_loop(0, TIMES, functools.partial(combine, core, a), 0, unroll=2)
+        lax.fori_loop(0, TIMES, functools.partial(combine, core, a), 0, unroll=4)
         swaps[a].wait_recv()
         from_core[a] = from_core[a] + sums[core, a]
         sends = []

time: 66 us -> 65.7 us (level)
  no operation moved by 1% of the time
where the time goes in v8:
time: 65.7 us; the launch traced here: 65.5 us
  Pallas kernels  63.1 us (96%)
  local copies, waits for them, and re-layouts  1.67 us (3%)
  between operations  0.66 us (1%)
    pallas_call x1, Pallas kernels, body(): pl.pallas_call(kernel, out_shape=jax.ShapeDtypeStruct((1, N_POT, N_POT),...  63.1 us
    unnamed x1, local copies, waits for them, and re-layouts  1.67 us

profile of v8, /device:TPU:1, one launch (start us, length us, event | category | flops | bytes accessed | tf_op | source)
XLA Modules:
  0.0 65.5 jit_solution(88401846289503562)
XLA Ops:
  0.7 63.1 %shard_map.73 = f32[1,256,256]{2,1,0:T(8,128)} custom-call(bf16[384,2048]{1,0:T(8,128)(2,1)} %occ_ref.1, bf16[384,4096]{1,0:T(8,128)(2,1)} %virt_ref.1, bf16[384,256]{1,0:T(8,128)(2,1)} %pot_ref.1, f32[1,2048]{1,0:T(1,128)} %bitcast.4, f32[1,4096]{1,0:T(1,128)} %bitcast.3, f32[1]{0:T(128)S(6)} %copy.9.times_ref, f32[1,8]{1,0:T(1,128)} %bitcast.5), custom_call_target="tpu_custom_call" | custom-call | tf_op jit(solution)/shard_map/pallas_call | solution.py:370
  63.8 1.7 %copy.10 = f32[1,256,256]{2,1,0:T(8,128)} copy(f32[1,256,256]{2,1,0:T(8,128)} %shard_map.73) | data formatting | bytes 524288
